TPU v7x, 32 devices: a whole 2x2x4 slice. The times are simulated.
32 devices in a mesh: batch: 4 (over z), seq: 8 (over y, x, core).
Axes of the slice: x: 2, y: 2, z: 4, core: 2. Of those that a mesh axis runs over, the one named last changes fastest.
Arguments:
- inputs: float32 [4, 1536, 512], P('batch', 'seq'), may hold values from -6 to 6
- cotangent: float32 [4, 1536, 512], P('batch', 'seq'), may hold values from -6 to 6
- full_gain_attn: float32 [512], replicated, may hold values from 0.5 to 1.5
- full_query: bfloat16 [512, 512], replicated, may hold values from -0.25 to 0.25
- full_key: bfloat16 [512, 512], replicated, may hold values from -0.25 to 0.25
- full_value: bfloat16 [512, 512], replicated, may hold values from -0.25 to 0.25
- full_output: bfloat16 [512, 512], replicated, may hold values from -2.5 to 2.5
- full_gain_ffn: float32 [512], replicated, may hold values from 0.5 to 1.5
- full_expand: bfloat16 [512, 2048], replicated, may hold values from -0.25 to 0.25
- full_contract: bfloat16 [2048, 512], replicated, may hold values from -0.125 to 0.125
- short_gain_attn: float32 [512], replicated, may hold values from 0.5 to 1.5
- short_query: bfloat16 [512, 512], replicated, may hold values from -0.25 to 0.25
- short_key: bfloat16 [512, 512], replicated, may hold values from -0.25 to 0.25
- short_value: bfloat16 [512, 512], replicated, may hold values from -0.25 to 0.25
- short_output: bfloat16 [512, 512], replicated, may hold values from -1.5 to 1.5
- short_gain_ffn: float32 [512], replicated, may hold values from 0.5 to 1.5
- short_expand: bfloat16 [512, 2048], replicated, may hold values from -0.25 to 0.25
- short_contract: bfloat16 [2048, 512], replicated, may hold values from -0.125 to 0.125
Outputs:
- output: float32 [4, 1536, 512], P('batch', 'seq')
- input_grad: float32 [4, 1536, 512], P('batch', 'seq')
- grad_full_gain_attn: float32 [512], replicated
- grad_full_query: float32 [512, 512], replicated
- grad_full_key: float32 [512, 512], replicated
- grad_full_value: float32 [512, 512], replicated
- grad_full_output: float32 [512, 512], replicated
- grad_full_gain_ffn: float32 [512], replicated
- grad_full_expand: float32 [512, 2048], replicated
- grad_full_contract: float32 [2048, 512], replicated
- grad_short_gain_attn: float32 [512], replicated
- grad_short_query: float32 [512, 512], replicated
- grad_short_key: float32 [512, 512], replicated
- grad_short_value: float32 [512, 512], replicated
- grad_short_output: float32 [512, 512], replicated
- grad_short_gain_ffn: float32 [512], replicated
- grad_short_expand: float32 [512, 2048], replicated
- grad_short_contract: float32 [2048, 512], replicated
All inputs are finite; a program needn't handle non-finite values.
Results may differ from a plain program's by a relative error of at most 0.025.
Values may be sent and summed in bfloat16 or wider, within the bound.
No kernel may reach another device: no remote copies, remote signals or barrier semaphores. Data moves between devices by JAX's collectives and lax.ppermute only.
A program may use at most 384 MiB of HBM per device.

v0:
```python
from functools import partial

import jax
import jax.numpy as jnp
from jax import lax
from jax.sharding import PartitionSpec as P

HEADS = 8
HEAD = 64


norm_eps = 1e-05


def from_behind(block, axis, distance):
    devices = range(lax.axis_size(axis))
    route = [(i - distance, i) for i in devices if i - distance in devices]
    return lax.ppermute(block, axis, route)


def normalize(stream, gain):
    row_mean = jnp.mean(stream, axis=-1, keepdims=True)
    centered = stream - row_mean
    spread = jnp.mean(centered * centered, axis=-1, keepdims=True)
    return centered * lax.rsqrt(spread + norm_eps) * gain


def rope_table(positions):
    half_size = HEAD // 2
    frequency = jnp.power(10000.0, -jnp.arange(half_size, dtype=jnp.float32) * 2.0 / HEAD)
    angles = positions.astype(jnp.float32)[:, None] * frequency[None, :]
    return (jnp.cos(angles)[:, None, :], jnp.sin(angles)[:, None, :])


def rotate(values, angle_cos, angle_sin):
    first_half, second_half = jnp.split(values, 2, axis=-1)
    return jnp.concatenate(
        [
            first_half * angle_cos - second_half * angle_sin,
            first_half * angle_sin + second_half * angle_cos,
        ],
        axis=-1,
    )


def rotate_back(grads, angle_cos, angle_sin):
    first_half, second_half = jnp.split(grads, 2, axis=-1)
    return jnp.concatenate(
        [
            first_half * angle_cos + second_half * angle_sin,
            second_half * angle_cos - first_half * angle_sin,
        ],
        axis=-1,
    )


def split_heads(matrix):
    return matrix.reshape(matrix.shape[0], HEADS, HEAD)


def project(stream, params, angle_cos, angle_sin):
    normed_in = normalize(stream, params[0]).astype(jnp.bfloat16)

    def heads_of(matrix):
        return split_heads(jnp.dot(normed_in, matrix, preferred_element_type=jnp.float32))

    queries = rotate(heads_of(params[1]), angle_cos, angle_sin).astype(jnp.bfloat16)
    keys_here = rotate(heads_of(params[2]), angle_cos, angle_sin).astype(jnp.bfloat16)
    values_here = heads_of(params[3]).astype(jnp.bfloat16)
    return (normed_in, queries, keys_here, values_here)


def masked_scores(queries, keys_all, query_places, key_places):
    scores = jnp.einsum(
        "nhe,mhe->hnm", queries, keys_all, preferred_element_type=jnp.float32
    ) * HEAD ** (-0.5)
    allowed = key_places[None, None, :] <= query_places[None, :, None]
    return jnp.where(allowed, scores, -1e30)


def attend(queries, keys_all, values_all, query_places, key_places):
    scores = masked_scores(queries, keys_all, query_places, key_places)
    highest_score = jnp.max(scores, axis=-1, keepdims=True)
    log_total = highest_score + jnp.log(
        jnp.sum(jnp.exp(scores - highest_score), axis=-1, keepdims=True)
    )
    prob_low = jnp.exp(scores - log_total).astype(jnp.bfloat16)
    attended = jnp.einsum("hnm,mhe->nhe", prob_low, values_all, preferred_element_type=jnp.float32)
    return (attended, log_total)


def attend_back(queries, keys_all, values_all, query_places, key_places, log_total, grad_attended):
    scores = masked_scores(queries, keys_all, query_places, key_places)
    probs_full = jnp.exp(scores - log_total)
    grad_probs = jnp.einsum(
        "nhe,mhe->hnm", grad_attended, values_all, preferred_element_type=jnp.float32
    )
    row_inner = jnp.sum(probs_full * grad_probs, axis=-1, keepdims=True)
    grad_scores = (probs_full * (grad_probs - row_inner)).astype(jnp.bfloat16)
    grad_queries = jnp.einsum(
        "hnm,mhe->nhe", grad_scores, keys_all, preferred_element_type=jnp.float32
    ) * HEAD ** (-0.5)
    return (grad_queries, grad_scores, probs_full.astype(jnp.bfloat16), row_inner)


def finish(stream, attended, params):
    row_count, width = stream.shape
    attended_low = attended.reshape(row_count, width).astype(jnp.bfloat16)
    middle = stream + jnp.dot(attended_low, params[4], preferred_element_type=jnp.float32)
    normed_mid = normalize(middle, params[5]).astype(jnp.bfloat16)
    hidden_pre = jnp.dot(normed_mid, params[6], preferred_element_type=jnp.float32)
    hidden_low = jax.nn.gelu(hidden_pre, approximate=True).astype(jnp.bfloat16)
    result = middle + jnp.dot(hidden_low, params[7], preferred_element_type=jnp.float32)
    return (result, (attended_low, middle, normed_mid, hidden_pre, hidden_low))


def finish_back(grad_result, finish_saved, params):
    attended_low, middle, normed_mid, hidden_pre, hidden_low = finish_saved
    grad_low = grad_result.astype(jnp.bfloat16)
    grad_contract = jnp.einsum(
        "nf,nd->fd", hidden_low, grad_low, preferred_element_type=jnp.float32
    )
    grad_hidden = jnp.einsum("nd,fd->nf", grad_low, params[7], preferred_element_type=jnp.float32)
    gelu_value, gelu_pull = jax.vjp(partial(jax.nn.gelu, approximate=True), hidden_pre)
    grad_pre = gelu_pull(grad_hidden)[0].astype(jnp.bfloat16)
    grad_expand = jnp.einsum("nd,nf->df", normed_mid, grad_pre, preferred_element_type=jnp.float32)
    grad_normed = jnp.einsum("nf,df->nd", grad_pre, params[6], preferred_element_type=jnp.float32)
    norm_value, norm_pull = jax.vjp(normalize, middle, params[5])
    grad_norm_in, grad_gain_ffn = norm_pull(grad_normed)
    grad_middle = grad_result + grad_norm_in
    middle_low = grad_middle.astype(jnp.bfloat16)
    grad_output_w = jnp.einsum(
        "nc,nd->cd", attended_low, middle_low, preferred_element_type=jnp.float32
    )
    grad_attended = split_heads(
        jnp.einsum("nd,cd->nc", middle_low, params[4], preferred_element_type=jnp.float32).astype(
            jnp.bfloat16
        )
    )
    return (grad_middle, grad_attended, grad_output_w, grad_expand, grad_contract, grad_gain_ffn)


def start_back(
    grad_queries, grad_keys, grad_values, stream, params, normed_in, angle_cos, angle_sin
):
    row_count, width = stream.shape
    query_low = (
        rotate_back(grad_queries, angle_cos, angle_sin)
        .reshape(row_count, width)
        .astype(jnp.bfloat16)
    )
    key_low = (
        rotate_back(grad_keys, angle_cos, angle_sin).reshape(row_count, width).astype(jnp.bfloat16)
    )
    value_low = grad_values.reshape(row_count, width).astype(jnp.bfloat16)
    grad_query = jnp.einsum("nd,nc->dc", normed_in, query_low, preferred_element_type=jnp.float32)
    grad_key = jnp.einsum("nd,nc->dc", normed_in, key_low, preferred_element_type=jnp.float32)
    grad_value = jnp.einsum("nd,nc->dc", normed_in, value_low, preferred_element_type=jnp.float32)
    grad_normed = (
        jnp.einsum("nc,dc->nd", query_low, params[1], preferred_element_type=jnp.float32)
        + jnp.einsum("nc,dc->nd", key_low, params[2], preferred_element_type=jnp.float32)
        + jnp.einsum("nc,dc->nd", value_low, params[3], preferred_element_type=jnp.float32)
    )
    norm_value, norm_pull = jax.vjp(normalize, stream, params[0])
    grad_stream, grad_gain_attn = norm_pull(grad_normed)
    return (grad_stream, grad_gain_attn, grad_query, grad_key, grad_value)


def local_forward(stream, places, params, fetch):
    angle_cos, angle_sin = rope_table(places)
    normed_in, queries, keys_here, values_here = project(stream, params, angle_cos, angle_sin)
    row_count, width = stream.shape
    keys_local = keys_here.reshape(row_count, width)
    values_local = values_here.reshape(row_count, width)
    keys_flat, values_flat = fetch(keys_local, values_local)
    key_places = jnp.arange(keys_flat.shape[0], dtype=jnp.int32)
    attended, log_total = attend(
        queries, split_heads(keys_flat), split_heads(values_flat), places, key_places
    )
    result, finish_saved = finish(stream, attended, params)
    return (
        result,
        (
            normed_in,
            queries,
            keys_local,
            values_local,
            keys_flat,
            values_flat,
            log_total,
            angle_cos,
            angle_sin,
            finish_saved,
        ),
    )


def local_backward(grad_result, stream, places, params, saved, keys_flat, values_flat, key_sum):
    normed_in, queries = (saved[0], saved[1])
    log_total, angle_cos, angle_sin, finish_saved = (saved[6], saved[7], saved[8], saved[9])
    grad_middle, grad_attended, grad_output_w, grad_expand, grad_contract, grad_gain_ffn = (
        finish_back(grad_result, finish_saved, params)
    )
    row_count, width = stream.shape
    key_places = jnp.arange(keys_flat.shape[0], dtype=jnp.int32)
    grad_queries, grad_scores, prob_low, row_inner = attend_back(
        queries,
        split_heads(keys_flat),
        split_heads(values_flat),
        places,
        key_places,
        log_total,
        grad_attended,
    )

    def contribution(first_row, term_rows):
        grad_keys = jnp.einsum(
            "hnm,nhe->mhe", grad_scores, queries, preferred_element_type=jnp.float32
        ) * HEAD ** (-0.5)
        grad_values = jnp.einsum(
            "hnm,nhe->mhe", prob_low, grad_attended, preferred_element_type=jnp.float32
        )
        return jnp.concatenate(
            [grad_keys.reshape(term_rows, width), grad_values.reshape(term_rows, width)], axis=1
        )

    both_grads = key_sum(contribution, row_count, (queries, grad_attended, log_total, row_inner))
    grad_stream, grad_gain_attn, grad_query, grad_key, grad_value = start_back(
        grad_queries,
        split_heads(both_grads[:, :width]),
        split_heads(both_grads[:, width:]),
        stream,
        params,
        normed_in,
        angle_cos,
        angle_sin,
    )
    return (
        grad_middle + grad_stream,
        (
            grad_gain_attn,
            grad_query,
            grad_key,
            grad_value,
            grad_output_w,
            grad_gain_ffn,
            grad_expand,
            grad_contract,
        ),
    )


def whole_forward(stream, params):
    row_count, width = stream.shape
    places = jnp.arange(row_count, dtype=jnp.int32)
    angle_cos, angle_sin = rope_table(places)
    normed_in, queries, keys_here, values_here = project(stream, params, angle_cos, angle_sin)
    block_rows = 512
    block_count = row_count // block_rows

    def one_block(pieces):
        return attend(pieces[0], keys_here, values_here, pieces[1], places)

    attended, log_total = lax.map(
        one_block,
        (
            queries.reshape(block_count, block_rows, HEADS, HEAD),
            places.reshape(block_count, block_rows),
        ),
    )
    result, finish_saved = finish(stream, attended.reshape(row_count, HEADS, HEAD), params)
    return (
        result,
        (normed_in, queries, keys_here, values_here, log_total, angle_cos, angle_sin, finish_saved),
    )


def whole_backward(grad_result, stream, params, saved):
    normed_in, queries, keys_here, values_here, log_total, angle_cos, angle_sin, finish_saved = (
        saved
    )
    grad_middle, grad_attended, grad_output_w, grad_expand, grad_contract, grad_gain_ffn = (
        finish_back(grad_result, finish_saved, params)
    )
    row_count, width = stream.shape
    places = jnp.arange(row_count, dtype=jnp.int32)
    block_rows = 512
    block_count = row_count // block_rows

    def one_block(running, pieces):
        query_block, place_block, total_block, grad_block = pieces
        grad_queries, grad_scores, prob_low, row_inner = attend_back(
            query_block, keys_here, values_here, place_block, places, total_block, grad_block
        )
        grad_keys = running[0] + jnp.einsum(
            "hnm,nhe->mhe", grad_scores, query_block, preferred_element_type=jnp.float32
        ) * HEAD ** (-0.5)
        grad_values = running[1] + jnp.einsum(
            "hnm,nhe->mhe", prob_low, grad_block, preferred_element_type=jnp.float32
        )
        return ((grad_keys, grad_values), grad_queries)

    zero_grads = jnp.zeros((row_count, HEADS, HEAD), jnp.float32)
    (grad_keys, grad_values), grad_queries = lax.scan(
        one_block,
        (zero_grads, zero_grads),
        (
            queries.reshape(block_count, block_rows, HEADS, HEAD),
            places.reshape(block_count, block_rows),
            log_total,
            grad_attended.reshape(block_count, block_rows, HEADS, HEAD),
        ),
    )
    grad_stream, grad_gain_attn, grad_query, grad_key, grad_value = start_back(
        grad_queries.reshape(row_count, HEADS, HEAD),
        grad_keys,
        grad_values,
        stream,
        params,
        normed_in,
        angle_cos,
        angle_sin,
    )
    return (
        grad_middle + grad_stream,
        (
            grad_gain_attn,
            grad_query,
            grad_key,
            grad_value,
            grad_output_w,
            grad_gain_ffn,
            grad_expand,
            grad_contract,
        ),
    )


def local(
    inputs,
    cotangent,
    full_gain_attn,
    full_query,
    full_key,
    full_value,
    full_output,
    full_gain_ffn,
    full_expand,
    full_contract,
    short_gain_attn,
    short_query,
    short_key,
    short_value,
    short_output,
    short_gain_ffn,
    short_expand,
    short_contract,
):
    full_params = (
        full_gain_attn,
        full_query,
        full_key,
        full_value,
        full_output,
        full_gain_ffn,
        full_expand,
        full_contract,
    )
    short_params = (
        short_gain_attn,
        short_query,
        short_key,
        short_value,
        short_output,
        short_gain_ffn,
        short_expand,
        short_contract,
    )
    stream_in = inputs[0]
    row_count, width = stream_in.shape
    own_short = row_count // 3
    position = lax.axis_index("seq")
    seq_parts = lax.axis_size("seq")
    places = position * row_count + jnp.arange(row_count, dtype=jnp.int32)

    def fetch_full(keys_local, values_local):
        return (
            lax.all_gather(keys_local, "seq", axis=0, tiled=True),
            lax.all_gather(values_local, "seq", axis=0, tiled=True),
        )

    residual, full_saved = local_forward(stream_in, places, full_params, fetch_full)
    tail_rows = from_behind(residual[row_count - 2 :], "seq", 1)
    shifted = jnp.concatenate([tail_rows, residual[: row_count - 2]], axis=0)
    pooled = jnp.mean(shifted.reshape(own_short, 3, width), axis=1)
    pooled_all = lax.all_gather(pooled, "seq", axis=0, tiled=True)
    short_all, short_saved = whole_forward(pooled_all, short_params)
    short_result = lax.dynamic_slice_in_dim(short_all, position * own_short, own_short, 0)
    output = residual + jnp.repeat(short_result, 3, axis=0)
    grad_output = cotangent[0]
    grad_short = jnp.sum(grad_output.reshape(own_short, 3, width), axis=1)
    grad_short_all = lax.all_gather(grad_short, "seq", axis=0, tiled=True)
    grad_pooled_all, short_grads = whole_backward(
        grad_short_all, pooled_all, short_params, short_saved
    )
    grad_pooled = lax.dynamic_slice_in_dim(grad_pooled_all, position * own_short, own_short, 0)
    short_grads = tuple(
        (
            lax.dynamic_slice_in_dim(
                gradient,
                position * (gradient.shape[0] // seq_parts),
                gradient.shape[0] // seq_parts,
                0,
            )
            for gradient in short_grads
        )
    )
    grad_shifted = jnp.repeat(grad_pooled / 3.0, 3, axis=0)
    carried = from_behind(grad_shifted[:2], "seq", -1)
    grad_residual = grad_output + jnp.concatenate([grad_shifted[2:], carried], axis=0)
    keys_flat, values_flat = (
        lax.all_gather(full_saved[2], "seq", axis=0, tiled=True),
        lax.all_gather(full_saved[3], "seq", axis=0, tiled=True),
    )

    def full_sum(contribution, term_rows, query_side):
        return lax.psum_scatter(
            contribution(jnp.int32(0), term_rows * lax.axis_size("seq")).astype(jnp.bfloat16),
            "seq",
            scatter_dimension=0,
            tiled=True,
        ).astype(jnp.float32)

    grad_input, full_grads = local_backward(
        grad_residual, stream_in, places, full_params, full_saved, keys_flat, values_flat, full_sum
    )
    full_shares = (
        lax.psum_scatter(
            full_grads[0].astype(jnp.bfloat16), "seq", scatter_dimension=0, tiled=True
        ).astype(jnp.float32),
        lax.psum_scatter(
            full_grads[1].astype(jnp.bfloat16), "seq", scatter_dimension=0, tiled=True
        ).astype(jnp.float32),
        lax.psum_scatter(
            full_grads[2].astype(jnp.bfloat16), "seq", scatter_dimension=0, tiled=True
        ).astype(jnp.float32),
        lax.psum_scatter(
            full_grads[3].astype(jnp.bfloat16), "seq", scatter_dimension=0, tiled=True
        ).astype(jnp.float32),
        lax.psum_scatter(
            full_grads[4].astype(jnp.bfloat16), "seq", scatter_dimension=0, tiled=True
        ).astype(jnp.float32),
        lax.psum_scatter(
            full_grads[5].astype(jnp.bfloat16), "seq", scatter_dimension=0, tiled=True
        ).astype(jnp.float32),
        lax.psum_scatter(
            full_grads[6].astype(jnp.bfloat16), "seq", scatter_dimension=0, tiled=True
        ).astype(jnp.float32),
        lax.psum_scatter(
            full_grads[7].astype(jnp.bfloat16), "seq", scatter_dimension=0, tiled=True
        ).astype(jnp.float32),
    )
    shares = tuple(full_shares) + tuple(short_grads)
    totals = (
        lax.psum(shares[0].astype(jnp.bfloat16), "batch").astype(jnp.float32),
        lax.psum(shares[1].astype(jnp.bfloat16), "batch").astype(jnp.float32),
        lax.psum(shares[2].astype(jnp.bfloat16), "batch").astype(jnp.float32),
        lax.psum(shares[3].astype(jnp.bfloat16), "batch").astype(jnp.float32),
        lax.psum(shares[4].astype(jnp.bfloat16), "batch").astype(jnp.float32),
        lax.psum(shares[5].astype(jnp.bfloat16), "batch").astype(jnp.float32),
        lax.psum(shares[6].astype(jnp.bfloat16), "batch").astype(jnp.float32),
        lax.psum(shares[7].astype(jnp.bfloat16), "batch").astype(jnp.float32),
        lax.psum(shares[8].astype(jnp.bfloat16), "batch").astype(jnp.float32),
        lax.psum(shares[9].astype(jnp.bfloat16), "batch").astype(jnp.float32),
        lax.psum(shares[10].astype(jnp.bfloat16), "batch").astype(jnp.float32),
        lax.psum(shares[11].astype(jnp.bfloat16), "batch").astype(jnp.float32),
        lax.psum(shares[12].astype(jnp.bfloat16), "batch").astype(jnp.float32),
        lax.psum(shares[13].astype(jnp.bfloat16), "batch").astype(jnp.float32),
        lax.psum(shares[14].astype(jnp.bfloat16), "batch").astype(jnp.float32),
        lax.psum(shares[15].astype(jnp.bfloat16), "batch").astype(jnp.float32),
    )
    whole = (
        lax.all_gather(totals[0].astype(jnp.bfloat16), "seq", axis=0, tiled=True).astype(
            jnp.float32
        ),
        lax.all_gather(totals[1].astype(jnp.bfloat16), "seq", axis=0, tiled=True).astype(
            jnp.float32
        ),
        lax.all_gather(totals[2].astype(jnp.bfloat16), "seq", axis=0, tiled=True).astype(
            jnp.float32
        ),
        lax.all_gather(totals[3].astype(jnp.bfloat16), "seq", axis=0, tiled=True).astype(
            jnp.float32
        ),
        lax.all_gather(totals[4].astype(jnp.bfloat16), "seq", axis=0, tiled=True).astype(
            jnp.float32
        ),
        lax.all_gather(totals[5].astype(jnp.bfloat16), "seq", axis=0, tiled=True).astype(
            jnp.float32
        ),
        lax.all_gather(totals[6].astype(jnp.bfloat16), "seq", axis=0, tiled=True).astype(
            jnp.float32
        ),
        lax.all_gather(totals[7].astype(jnp.bfloat16), "seq", axis=0, tiled=True).astype(
            jnp.float32
        ),
        lax.all_gather(totals[8].astype(jnp.bfloat16), "seq", axis=0, tiled=True).astype(
            jnp.float32
        ),
        lax.all_gather(totals[9].astype(jnp.bfloat16), "seq", axis=0, tiled=True).astype(
            jnp.float32
        ),
        lax.all_gather(totals[10].astype(jnp.bfloat16), "seq", axis=0, tiled=True).astype(
            jnp.float32
        ),
        lax.all_gather(totals[11].astype(jnp.bfloat16), "seq", axis=0, tiled=True).astype(
            jnp.float32
        ),
        lax.all_gather(totals[12].astype(jnp.bfloat16), "seq", axis=0, tiled=True).astype(
            jnp.float32
        ),
        lax.all_gather(totals[13].astype(jnp.bfloat16), "seq", axis=0, tiled=True).astype(
            jnp.float32
        ),
        lax.all_gather(totals[14].astype(jnp.bfloat16), "seq", axis=0, tiled=True).astype(
            jnp.float32
        ),
        lax.all_gather(totals[15].astype(jnp.bfloat16), "seq", axis=0, tiled=True).astype(
            jnp.float32
        ),
    )
    return (output[None], grad_input[None]) + tuple(whole)


def solution(mesh):
    in_specs = (
        P("batch", "seq", None),
        P("batch", "seq", None),
        P(),
        P(),
        P(),
        P(),
        P(),
        P(),
        P(),
        P(),
        P(),
        P(),
        P(),
        P(),
        P(),
        P(),
        P(),
        P(),
    )
    out_specs = (
        P("batch", "seq", None),
        P("batch", "seq", None),
        P(),
        P(),
        P(),
        P(),
        P(),
        P(),
        P(),
        P(),
        P(),
        P(),
        P(),
        P(),
        P(),
        P(),
        P(),
        P(),
    )
    return jax.shard_map(local, mesh=mesh, in_specs=in_specs, out_specs=out_specs, check_vma=False)
```

profile of v0, /device:TPU:0, one launch (start us, length us, event | category | flops | bytes accessed | tf_op | source)
XLA Modules:
  0.0 748.0 jit_solution(8848777497394496225)
XLA Ops:
  20.3 26.8 %all-gather.11.cloned.1.call-done = bf16[1536,512]{1,0:T(8,128)(2,1)} async-done(((bf16[192,512]{1,0:T(8,128)(2,1)}), bf16[1536,512]{1,0:T(8,128)(2,1)}) %all-gather.11.cloned.1.call-update) | async-done | bytes 1572880 | tf_op jit(solution)/shard_map/all_gather | solution.py:388
  56.6 18.7 %all-gather.9.cloned.1.call-done = bf16[1536,512]{1,0:T(8,128)(2,1)} async-done(((bf16[192,512]{1,0:T(8,128)(2,1)}), bf16[1536,512]{1,0:T(8,128)(2,1)}) %all-gather.9.cloned.1.call-update) | async-done | bytes 1572880 | tf_op jit(solution)/shard_map/all_gather | solution.py:389
  77.9 6.7 convolution_convert_fusion.11
  99.5 22.1 %all-gather.13.cloned.1.call-done = f32[512,512]{1,0:T(8,128)} async-done(((f32[64,512]{1,0:T(8,128)}), f32[512,512]{1,0:T(8,128)}) %all-gather.13.cloned.1.call-update) | async-done | bytes 1048592 | tf_op jit(solution)/shard_map/all_gather | solution.py:396
  142.0 4.8 all-gather.15.cloned.1.call-done
  146.8 6.9 fusion.10
  157.3 6.1 convolution_convert_fusion.3
  185.7 6.4 convolution_convert_fusion.2
  192.1 6.1 multiply_reduce_fusion
  206.1 4.7 copy.69
  225.2 34.7 %reduce-scatter.22.cloned.1.call-done = bf16[192,1024]{1,0:T(8,128)(2,1)} async-done(((bf16[1536,1024]{1,0:T(8,128)(2,1)}), bf16[192,1024]{1,0:T(8,128)(2,1)}) %reduce-scatter.22.cloned.1.call-update) | async-done | bytes 393232
  268.0 5.5 fusion.26
  281.7 16.2 %reduce-scatter.16.cloned.1.call-done = bf16[64,512]{1,0:T(8,128)(2,1)} async-done(((bf16[512,512]{1,0:T(8,128)(2,1)}), bf16[64,512]{1,0:T(8,128)(2,1)}) %reduce-scatter.16.cloned.1.call-update) | async-done | bytes 65552 | tf_op jit(solution)/shard_map/reduce_scatter | solution.py:450
  297.9 45.1 %reduce-scatter.20.cloned.1.call-done = bf16[256,512]{1,0:T(8,128)(2,1)} async-done(((bf16[2048,512]{1,0:T(8,128)(2,1)}), bf16[256,512]{1,0:T(8,128)(2,1)}) %reduce-scatter.20.cloned.1.call-update) | async-done | bytes 262160 | tf_op jit(solution)/shard_map/reduce_scatter | solution.py:459
  343.0 45.5 %reduce-scatter.18.cloned.1.call-done = bf16[64,2048]{1,0:T(8,128)(2,1)} async-done(((bf16[512,2048]{1,0:T(8,128)(2,1)}), bf16[64,2048]{1,0:T(8,128)(2,1)}) %reduce-scatter.18.cloned.1.call-update) | async-done | bytes 262160 | tf_op jit(solution)/shard_map/reduce_scatter | solution.py:456
  388.5 37.8 %reduce-scatter.14.cloned.1.call-done = bf16[64,512]{1,0:T(8,128)(2,1)} async-done(((bf16[512,512]{1,0:T(8,128)(2,1)}), bf16[64,512]{1,0:T(8,128)(2,1)}) %reduce-scatter.14.cloned.1.call-update) | async-done | bytes 65552 | tf_op jit(solution)/shard_map/reduce_scatter | solution.py:447
  426.3 38.0 %reduce-scatter.12.cloned.1.call-done = bf16[64,512]{1,0:T(8,128)(2,1)} async-done(((bf16[512,512]{1,0:T(8,128)(2,1)}), bf16[64,512]{1,0:T(8,128)(2,1)}) %reduce-scatter.12.cloned.1.call-update) | async-done | bytes 65552 | tf_op jit(solution)/shard_map/reduce_scatter | solution.py:444
  464.3 37.8 %reduce-scatter.10.cloned.1.call-done = bf16[64,512]{1,0:T(8,128)(2,1)} async-done(((bf16[512,512]{1,0:T(8,128)(2,1)}), bf16[64,512]{1,0:T(8,128)(2,1)}) %reduce-scatter.10.cloned.1.call-update) | async-done | bytes 65552 | tf_op jit(solution)/shard_map/reduce_scatter | solution.py:441
  502.2 77.6 %all-reduce.12.cloned.1.call-done = (bf16[64,512]{1,0:T(8,128)(2,1)}, bf16[64,512]{1,0:T(8,128)(2,1)}, bf16[64,512]{1,0:T(8,128)(2,1)}, bf16[64,512]{1,0:T(8,128...) async-done(((bf16[64,512]{1,0:T(8,128)(2,1)}, ...) | async-done | bytes 1572880 | tf_op jit(solution)/shard_map/psum | solution.py:466
  583.5 4.3 fusion.66
  594.2 13.9 %all-reduce.7 = (bf16[512]{0:T(512)(128)(2,1)S(1)}, bf16[512]{0:T(512)(128)(2,1)S(1)}) all-reduce(bf16[512]{0:T(512)(128)(2,1)S(1)} %get-tuple-element.81, bf16[512]{0:T(512)(128)(2,1)S(1)} %get-tuple-element.79), channel_id=3, replica_groups=mesh['batch'=4,'seq'=8] {'seq'}, use_global_device_ids=true, to_apply=%region_26.27.clone | all-reduce | flops 1024 | bytes 4096
  608.2 9.6 %all-reduce.8 = (bf16[64]{0:T(256)(128)(2,1)S(1)}, bf16[64]{0:T(256)(128)(2,1)S(1)}, bf16[64]{0:T(256)(128)(2,1)S(1)}, bf16[64]{0:T(256)(128)(2,1)S(1)}) all-reduce(bf16[64]{0:T(256)(128)(2,1)S(1)} %dynamic-slice.11, bf16[64]{0:T(256)(128)(2,1)S(1)} %dynamic-slice.13, ...), channel_id=1, replica_groups=mesh['batch'=4,'seq'=8] {'batch'}, use_global_device_ids=true, to_apply=%region_27.28 | all-reduce | flops 256 | bytes 1024 | tf_op jit(solution)/shard_map/psum | solution.py:465
  618.7 11.9 %all-reduce.6 = (bf16[512]{0:T(512)(128)(2,1)S(1)}, bf16[512]{0:T(512)(128)(2,1)S(1)}, bf16[512]{0:T(512)(128)(2,1)S(1)}, bf16[512]{0:T(512)(128)(2,1)S(1)}) all-reduce(bf16[512]{0:T(512)(128)(2,1)S(1)} %dynamic-update-slice, bf16[512]{0:T(512)(128)(2,1)S(1)} %dynamic-update-slice.1, ...), channel_id=1, replica_groups=mesh['batch'=4,'seq'=8] {'seq'}, use_global_device_ids=true, to_apply=%add | all-reduce | flops 2048 | bytes 8192
  634.1 9.3 %all_gather.67 = bf16[512,512]{1,0:T(8,128)(2,1)S(1)} all-gather(bf16[64,512]{1,0:T(8,128)(2,1)S(1)} %copy-done.95), channel_id=1, replica_groups=mesh['batch'=4,'seq'=8] {'seq'}, dimensions={0}, use_global_device_ids=true | all-gather | bytes 589824 | tf_op jit(solution)/shard_map/all_gather | solution.py:486
  644.5 11.4 %all_gather.68 = bf16[512,512]{1,0:T(8,128)(2,1)S(1)} all-gather(bf16[64,512]{1,0:T(8,128)(2,1)S(1)} %copy-done.94), channel_id=1, replica_groups=mesh['batch'=4,'seq'=8] {'seq'}, dimensions={0}, use_global_device_ids=true | all-gather | bytes 589824 | tf_op jit(solution)/shard_map/all_gather | solution.py:489
  657.0 11.2 %all_gather.69 = bf16[512,512]{1,0:T(8,128)(2,1)S(1)} all-gather(bf16[64,512]{1,0:T(8,128)(2,1)S(1)} %copy-done.93), channel_id=1, replica_groups=mesh['batch'=4,'seq'=8] {'seq'}, dimensions={0}, use_global_device_ids=true | all-gather | bytes 589824 | tf_op jit(solution)/shard_map/all_gather | solution.py:492
  669.2 9.7 %all_gather.70 = bf16[512,512]{1,0:T(8,128)(2,1)S(1)} all-gather(bf16[64,512]{1,0:T(8,128)(2,1)S(1)} %copy-done.92), channel_id=1, replica_groups=mesh['batch'=4,'seq'=8] {'seq'}, dimensions={0}, use_global_device_ids=true | all-gather | bytes 589824 | tf_op jit(solution)/shard_map/all_gather | solution.py:495
  680.0 9.8 %all_gather.75 = bf16[512,512]{1,0:T(8,128)(2,1)S(1)} all-gather(bf16[64,512]{1,0:T(8,128)(2,1)S(1)} %copy-done.91), channel_id=1, replica_groups=mesh['batch'=4,'seq'=8] {'seq'}, dimensions={0}, use_global_device_ids=true | all-gather | bytes 589824 | tf_op jit(solution)/shard_map/all_gather | solution.py:510
  690.9 11.3 %all_gather.76 = bf16[512,512]{1,0:T(8,128)(2,1)S(1)} all-gather(bf16[64,512]{1,0:T(8,128)(2,1)S(1)} %copy-done.90), channel_id=1, replica_groups=mesh['batch'=4,'seq'=8] {'seq'}, dimensions={0}, use_global_device_ids=true | all-gather | bytes 589824 | tf_op jit(solution)/shard_map/all_gather | solution.py:513
  703.3 9.7 %all_gather.77 = bf16[512,512]{1,0:T(8,128)(2,1)S(1)} all-gather(bf16[64,512]{1,0:T(8,128)(2,1)S(1)} %copy-done.89), channel_id=1, replica_groups=mesh['batch'=4,'seq'=8] {'seq'}, dimensions={0}, use_global_device_ids=true | all-gather | bytes 589824 | tf_op jit(solution)/shard_map/all_gather | solution.py:516
  714.2 9.0 %all_gather.78 = bf16[512,512]{1,0:T(8,128)(2,1)S(1)} all-gather(bf16[64,512]{1,0:T(8,128)(2,1)S(1)} %copy-done.88), channel_id=1, replica_groups=mesh['batch'=4,'seq'=8] {'seq'}, dimensions={0}, use_global_device_ids=true | all-gather | bytes 589824 | tf_op jit(solution)/shard_map/all_gather | solution.py:519
  732.6 4.3 convert_element_type.393
  (467 shorter events, 157.6 us)
Async XLA Ops:
  7.2 131.4 %copy-start = (bf16[512,2048]{1,0:T(8,128)(2,1)S(1)}, bf16[512,2048]{1,0:T(8,128)(2,1)}, u32[]{:S(2)}) copy-start(bf16[512,2048]{1,0:T(8,128)(2,1)} %param.34) | copy-start | bytes 6291460
  7.2 39.9 %all-gather.11.cloned.1.call-start = ((), (), s32[]{:S(2)}) async-start(), calls=%async_computation.8 | async-start | bytes 1769472 | tf_op jit(solution)/shard_map/all_gather | solution.py:388
  18.5 56.7 %all-gather.9.cloned.1.call-start = ((), (), s32[]{:S(2)}) async-start(), calls=%async_computation.7 | async-start | bytes 1769472 | tf_op jit(solution)/shard_map/all_gather | solution.py:389
  19.9 101.6 %all-gather.13.cloned.1.call-start = ((), (), s32[]{:S(2)}) async-start(), calls=%async_computation.9 | async-start | bytes 1179648 | tf_op jit(solution)/shard_map/all_gather | solution.py:396
  20.2 57.6 %copy-start.18 = (pred[192,1536]{1,0:T(8,128)(4,1)}, pred[192,1536]{1,0:T(8,128)(4,1)S(1)}, u32[]{:S(2)}) copy-start(pred[192,1536]{1,0:T(8,128)(4,1)S(1)} %iota_compare_fusion) | copy-start | bytes 884740
  87.2 3.1 collective-permute-start
  95.1 51.7 %all-gather.15.cloned.1.call-start = ((), (), s32[]{:S(2)}) async-start(), calls=%async_computation.10 | async-start | bytes 1179648 | tf_op jit(solution)/shard_map/all_gather | solution.py:402
  98.1 161.8 %reduce-scatter.22.cloned.1.call-start = ((), (), s32[]{:S(2)}) async-start(), calls=%async_computation.21 | async-start | bytes 3538944
  175.2 3.1 collective-permute-start.1
  210.8 87.0 %reduce-scatter.16.cloned.1.call-start = ((), (), s32[]{:S(2)}) async-start(), calls=%async_computation.14 | async-start | bytes 589824 | tf_op jit(solution)/shard_map/reduce_scatter | solution.py:450
  212.0 131.0 %reduce-scatter.20.cloned.1.call-start = ((), (), s32[]{:S(2)}) async-start(), calls=%async_computation.17 | async-start | bytes 2359296 | tf_op jit(solution)/shard_map/reduce_scatter | solution.py:459
  215.7 172.8 %reduce-scatter.18.cloned.1.call-start = ((), (), s32[]{:S(2)}) async-start(), calls=%async_computation.15 | async-start | bytes 2359296 | tf_op jit(solution)/shard_map/reduce_scatter | solution.py:456
  217.9 42.0 %copy-start.108 = (f32[192]{0:T(256)S(1)}, f32[192]{0:T(256)}, u32[]{:S(2)}) copy-start(f32[192]{0:T(256)} %copy-done.107) | copy-start | bytes 2308
  217.9 208.4 %reduce-scatter.14.cloned.1.call-start = ((), (), s32[]{:S(2)}) async-start(), calls=%async_computation.13 | async-start | bytes 589824 | tf_op jit(solution)/shard_map/reduce_scatter | solution.py:447
  218.2 44.0 %copy-start.12 = (bf16[1536,512]{0,1:T(8,128)(2,1)S(1)}, bf16[1536,512]{0,1:T(8,128)(2,1)}, u32[]{:S(2)}) copy-start(bf16[1536,512]{0,1:T(8,128)(2,1)} %copy.59) | copy-start | bytes 4718596
  262.2 202.1 %reduce-scatter.12.cloned.1.call-start = ((), (), s32[]{:S(2)}) async-start(), calls=%async_computation.12 | async-start | bytes 589824 | tf_op jit(solution)/shard_map/reduce_scatter | solution.py:444
  267.9 234.2 %reduce-scatter.10.cloned.1.call-start = ((), (), s32[]{:S(2)}) async-start(), calls=%async_computation.11 | async-start | bytes 589824 | tf_op jit(solution)/shard_map/reduce_scatter | solution.py:441
  274.7 305.1 %all-reduce.12.cloned.1.call-start = ((), (), s32[]{:S(2)}) async-start(), calls=%async_computation.22 | async-start | bytes 3145728 | tf_op jit(solution)/shard_map/psum | solution.py:466
  278.0 303.6 %copy-start.124 = (u32[32]{0:T(128)S(1)}, u32[32]{0:T(128)}, u32[]{:S(2)}) copy-start(u32[32]{0:T(128)} %constant.126) | copy-start | bytes 388
  502.1 222.1 %all-gather.23.cloned.1.call-start = ((), (), s32[]{:S(2)}) async-start(), calls=%async_computation.20 | async-start | bytes 2359296 | tf_op jit(solution)/shard_map/all_gather | solution.py:528
  579.8 148.7 %all-gather.21.cloned.1.call-start = ((), (), s32[]{:S(2)}) async-start(), calls=%async_computation.19 | async-start | bytes 2359296 | tf_op jit(solution)/shard_map/all_gather | solution.py:525
  580.4 152.2 %all-gather.19.cloned.1.call-start = ((), (), s32[]{:S(2)}) async-start(), calls=%async_computation.18 | async-start | bytes 2359296 | tf_op jit(solution)/shard_map/all_gather | solution.py:504
  581.0 156.0 %all-gather.17.cloned.1.call-start = ((), (), s32[]{:S(2)}) async-start(), calls=%async_computation.16 | async-start | bytes 2359296 | tf_op jit(solution)/shard_map/all_gather | solution.py:501
  587.8 45.1 %copy-start.121 = (f32[192]{0:T(256)S(1)}, f32[192]{0:T(256)}, u32[]{:S(2)}) copy-start(f32[192]{0:T(256)} %copy-done.120) | copy-start | bytes 2308
  587.9 45.3 %copy-start.24 = (f32[192,512]{1,0:T(8,128)S(1)}, f32[192,512]{1,0:T(8,128)}, u32[]{:S(2)}) copy-start(f32[192,512]{1,0:T(8,128)} %copy-done.23) | copy-start | bytes 1179652
  588.9 45.2 %copy-start.95 = (bf16[64,512]{1,0:T(8,128)(2,1)S(1)}, bf16[64,512]{1,0:T(8,128)(2,1)}, u32[]{:S(2)}) copy-start(bf16[64,512]{1,0:T(8,128)(2,1)} %get-tuple-element.93) | copy-start | bytes 196612
  592.4 52.1 %copy-start.94 = (bf16[64,512]{1,0:T(8,128)(2,1)S(1)}, bf16[64,512]{1,0:T(8,128)(2,1)}, u32[]{:S(2)}) copy-start(bf16[64,512]{1,0:T(8,128)(2,1)} %get-tuple-element.94) | copy-start | bytes 196612
  592.8 64.2 %copy-start.93 = (bf16[64,512]{1,0:T(8,128)(2,1)S(1)}, bf16[64,512]{1,0:T(8,128)(2,1)}, u32[]{:S(2)}) copy-start(bf16[64,512]{1,0:T(8,128)(2,1)} %get-tuple-element.95) | copy-start | bytes 196612
  634.1 45.9 %copy-start.91 = (bf16[64,512]{1,0:T(8,128)(2,1)S(1)}, bf16[64,512]{1,0:T(8,128)(2,1)}, u32[]{:S(2)}) copy-start(bf16[64,512]{1,0:T(8,128)(2,1)} %get-tuple-element.99) | copy-start | bytes 196612
  644.5 46.5 %copy-start.90 = (bf16[64,512]{1,0:T(8,128)(2,1)S(1)}, bf16[64,512]{1,0:T(8,128)(2,1)}, u32[]{:S(2)}) copy-start(bf16[64,512]{1,0:T(8,128)(2,1)} %get-tuple-element.100) | copy-start | bytes 196612
  656.9 46.4 %copy-start.89 = (bf16[64,512]{1,0:T(8,128)(2,1)S(1)}, bf16[64,512]{1,0:T(8,128)(2,1)}, u32[]{:S(2)}) copy-start(bf16[64,512]{1,0:T(8,128)(2,1)} %get-tuple-element.101) | copy-start | bytes 196612
  669.2 44.9 %copy-start.88 = (bf16[64,512]{1,0:T(8,128)(2,1)S(1)}, bf16[64,512]{1,0:T(8,128)(2,1)}, u32[]{:S(2)}) copy-start(bf16[64,512]{1,0:T(8,128)(2,1)} %get-tuple-element.102) | copy-start | bytes 196612
  (121 other events, 801.7 us)
Sparse Core Ops, SparseCore 0:
  18.6 28.3 all-gather.10
  49.5 25.6 all-gather.8
  95.2 26.2 all-gather.12
  123.3 23.4 all-gather.14
  211.0 48.9 reduce-scatter.21
  263.7 34.1 reduce-scatter.15
  301.8 41.1 reduce-scatter.19
  347.2 41.2 reduce-scatter.17
  392.2 34.1 reduce-scatter.13
  430.1 34.1 reduce-scatter.11
  468.0 34.1 reduce-scatter.9
  506.3 73.4 all-reduce.11
  581.8 26.6 all-gather.22
  610.4 27.8 all-gather.20
  640.2 30.4 all-gather.18
  672.6 30.3 all-gather.16
where the time goes:
time: 758 us; the launch traced here: 748 us
  waiting for transfers between devices  409 us (54%)
  blocking collectives  117 us (15%)
  matrix products  103 us (14%)
  other arithmetic  61.8 us (8%)
  local copies, waits for them, and re-layouts  35.2 us (5%)
  between operations  17.7 us (2%)
    psum x1, waiting for transfers between devices, local(): lax.psum(shares[1].astype(jnp.bfloat16), 'batch').astype(jnp.float32)  77.6 us
    reduce_scatter x1, waiting for transfers between devices, local(): lax.psum_scatter(full_grads[6].astype(jnp.bfloat16), 'seq', scatter_dimen...  45.5 us
    reduce_scatter x1, waiting for transfers between devices, local(): lax.psum_scatter(full_grads[7].astype(jnp.bfloat16), 'seq', scatter_dimen...  45.1 us
    reduce_scatter x1, waiting for transfers between devices, local(): lax.psum_scatter(full_grads[2].astype(jnp.bfloat16), 'seq', scatter_dimen...  38 us
    reduce_scatter x1, waiting for transfers between devices, local(): lax.psum_scatter(full_grads[3].astype(jnp.bfloat16), 'seq', scatter_dimen...  37.8 us
    reduce_scatter x1, waiting for transfers between devices, local(): lax.psum_scatter(full_grads[1].astype(jnp.bfloat16), 'seq', scatter_dimen...  37.8 us
    unnamed x17, waiting for transfers between devices  36.5 us
    all_gather x1, waiting for transfers between devices, fetch_full(): lax.all_gather(keys_local, 'seq', axis=0, tiled=True)  26.8 us
  transfers between devices with their start and end apart: 18, of which 14 were waited for; matrix products, arithmetic and copies ran while one was open for 14% of the time, Pallas kernels for 0%

commit v1 on v0

--- a/solution.py
+++ b/solution.py
@@ -2,14 +2,932 @@
 
 import jax
 import jax.numpy as jnp
+import numpy as np
 from jax import lax
+from jax.experimental import pallas as pl
+from jax.experimental.pallas import tpu as pltpu
 from jax.sharding import PartitionSpec as P
 
 HEADS = 8
 HEAD = 64
+LANES = 128
+BLOCK = 256
+F32 = jnp.float32
+BF16 = jnp.bfloat16
 
 
 norm_eps = 1e-05
+
+
+def dot_nn(left, right):
+    return jnp.dot(left, right, preferred_element_type=F32)
+
+
+def dot_nt(left, right):
+    return lax.dot_general(left, right, (((1,), (1,)), ((), ())), preferred_element_type=F32)
+
+
+def dot_tn(left, right):
+    return lax.dot_general(left, right, (((0,), (0,)), ((), ())), preferred_element_type=F32)
+
+
+def lower_half(rows):
+    return lax.broadcasted_iota(jnp.int32, (rows, LANES), 1) < HEAD
+
+
+def turn(values):
+    return pltpu.roll(values, HEAD, 1)
+
+
+def swap_pairs(values):
+    lane = lax.broadcasted_iota(jnp.int32, values.shape, 1)
+    return jnp.where(
+        lane % HEAD < HEAD // 2,
+        pltpu.roll(values, LANES - HEAD // 2, 1),
+        pltpu.roll(values, HEAD // 2, 1),
+    )
+
+
+def rope(values, table):
+    return values * table[:, :LANES] + swap_pairs(values) * table[:, LANES:]
+
+
+def rope_back(grads, table):
+    return grads * table[:, :LANES] - swap_pairs(grads) * table[:, LANES:]
+
+
+def rope_constants(rows):
+    frequency = np.power(
+        np.float32(10000.0), -np.arange(HEAD // 2, dtype=np.float32) * np.float32(2.0 / HEAD)
+    ).astype(np.float32)
+    angles = np.arange(rows, dtype=np.float32)[:, None] * frequency[None, :]
+    cosine, sine = np.cos(angles), np.sin(angles)
+    table = np.concatenate([cosine] * 4 + [-sine, sine] * 2, axis=1)
+    return jnp.asarray(table, F32)
+
+
+def norm_parts(stream):
+    centered = stream - jnp.mean(stream, axis=-1, keepdims=True)
+    spread = jnp.mean(centered * centered, axis=-1, keepdims=True)
+    scale = lax.rsqrt(spread + norm_eps)
+    return centered * scale, scale
+
+
+def norm_back(grad, gain, unit, scale):
+    grad_unit = grad * gain
+    inner = jnp.mean(grad_unit * unit, axis=-1, keepdims=True)
+    return scale * (grad_unit - jnp.mean(grad_unit, axis=-1, keepdims=True) - unit * inner)
+
+
+GELU_SCALE = 0.7978845608028654
+GELU_CUBE = 0.044715
+
+
+def gelu_both(pre):
+    square = pre * pre
+    tanh = jnp.tanh(GELU_SCALE * pre * (1.0 + GELU_CUBE * square))
+    half = 0.5 * (1.0 + tanh)
+    slope = half + 0.5 * pre * (1.0 - tanh * tanh) * (
+        GELU_SCALE * (1.0 + 3.0 * GELU_CUBE * square)
+    )
+    return pre * half, slope
+
+
+def gelu_value(pre):
+    tanh = jnp.tanh(GELU_SCALE * pre * (1.0 + GELU_CUBE * pre * pre))
+    return 0.5 * pre * (1.0 + tanh)
+
+
+def causal(scores, first_row, first_key):
+    row = lax.broadcasted_iota(jnp.int32, scores.shape, 0) + first_row
+    key = lax.broadcasted_iota(jnp.int32, scores.shape, 1) + first_key
+    return jnp.where(key <= row, scores, -1e30)
+
+
+def fold_rows(values):
+    half = values.shape[0] // 2
+    return jnp.where(lower_half(half), values[:half], turn(values[half:]))
+
+
+def unfold_rows(folded):
+    low = lower_half(folded.shape[0])
+    return jnp.where(low, folded, 0.0), jnp.where(low, turn(folded), 0.0)
+
+
+def rows_at(start, size, multiple):
+    return pl.ds(pl.multiple_of(start, multiple), size)
+
+
+def project_kernel(place, x, cot, gain, w_q, w_k, w_v, table, *refs):
+    pieces, bundle, heads, chunks = refs[:HEADS], refs[HEADS], refs[HEADS + 1], refs[HEADS + 2]
+    rows, width = x.shape
+    me = place[0]
+    unit, _ = norm_parts(x[...])
+    normed = (unit * gain[...]).astype(BF16)
+    own = table[rows_at(me * rows, rows, 16), :]
+    q = dot_nn(normed, w_q[...])
+    k = dot_nn(normed, w_k[...])
+    v = dot_nn(normed, w_v[...])
+    low = lower_half(rows)
+    low_half = lower_half(rows // 2)
+    for chunk in range(width // LANES):
+        cut = slice(chunk * LANES, (chunk + 1) * LANES)
+        q_chunk = rope(q[:, cut], own) * HEAD**-0.5
+        k_chunk = rope(k[:, cut], own)
+        v_chunk = v[:, cut]
+        first, later = q_chunk[: rows // 2], q_chunk[rows // 2 :]
+        heads[2 * chunk, :rows] = jnp.where(low, k_chunk, turn(v_chunk)).astype(BF16)
+        heads[2 * chunk + 1, :rows] = jnp.where(low, turn(k_chunk), v_chunk).astype(BF16)
+        heads[2 * chunk, rows:] = jnp.where(low_half, first, turn(later)).astype(BF16)
+        heads[2 * chunk + 1, rows:] = jnp.where(low_half, turn(first), later).astype(BF16)
+    for step in range(HEADS):
+        pieces[step][...] = heads[me ^ step]
+    bundle[:rows] = normed
+    bundle[rows : 2 * rows] = cot[...].astype(BF16)
+    for chunk in range(width // LANES):
+        cut = slice(chunk * LANES, (chunk + 1) * LANES)
+        chunks[chunk] = cot[:, cut]
+        total = sum(chunks[chunk, pl.ds(s, rows // 3, stride=3), :] for s in range(3))
+        bundle[2 * rows :, cut] = total.astype(BF16)
+
+
+def attend_kernel(place, *refs):
+    pieces, outs = refs[:HEADS], refs[HEADS : 2 * HEADS]
+    q_all, kv_all, lse_o = refs[2 * HEADS : 2 * HEADS + 3]
+    me = place[0]
+    rows = outs[0].shape[0] * 2
+    for step in range(HEADS):
+        start = (me ^ step) * rows
+        kv_all[rows_at(start, rows, 16), :] = pieces[step][:rows]
+        first, later = unfold_rows(pieces[step][rows:].astype(F32))
+        q_all[rows_at(start, rows // 2, 16), :] = first.astype(BF16)
+        q_all[rows_at(start + rows // 2, rows // 2, 16), :] = later.astype(BF16)
+    low = lower_half(BLOCK)
+    for block in range(q_all.shape[0] // BLOCK):
+        cut = slice(block * BLOCK, (block + 1) * BLOCK)
+        seen = kv_all[: (block + 1) * BLOCK]
+        scores = causal(dot_nt(q_all[cut], seen), block * BLOCK, 0)
+        most = jnp.max(scores, axis=-1, keepdims=True)
+        weights = jnp.exp(scores - most)
+        total = jnp.sum(weights, axis=-1, keepdims=True)
+        attended = dot_nn(weights.astype(BF16), seen) / total
+        lse_o[cut] = jnp.where(low, most + jnp.log(total), attended)
+    for step in range(HEADS):
+        own = lse_o[rows_at((me ^ step) * rows, rows, 16), :]
+        outs[step][...] = jnp.where(
+            lower_half(rows // 2), turn(own[: rows // 2]), own[rows // 2 :]
+        ).astype(BF16)
+
+
+def finish_kernel(place, x, gain, w_o, w_e, w_c, *refs):
+    pieces = refs[:HEADS]
+    result_out, middle_out, att_out, normed_out, pooled_out, heads, chunks = refs[HEADS:]
+    rows, width = x.shape
+    me = place[0]
+    for step in range(HEADS):
+        heads[me ^ step] = pieces[step][...].astype(F32)
+    low = lower_half(rows // 2)
+    for chunk in range(width // LANES):
+        cut = slice(chunk * LANES, (chunk + 1) * LANES)
+        even, odd = heads[2 * chunk], heads[2 * chunk + 1]
+        att_out[: rows // 2, cut] = jnp.where(low, even, turn(odd)).astype(BF16)
+        att_out[rows // 2 :, cut] = jnp.where(low, turn(even), odd).astype(BF16)
+    middle = x[...] + dot_nn(att_out[...], w_o[...])
+    middle_out[...] = middle
+    unit, _ = norm_parts(middle)
+    normed = (unit * gain[...]).astype(BF16)
+    normed_out[...] = normed
+    hidden = gelu_value(dot_nn(normed, w_e[...])).astype(BF16)
+    result = middle + dot_nn(hidden, w_c[...])
+    result_out[...] = result
+    short = rows // 3
+    for chunk in range(width // LANES):
+        cut = slice(chunk * LANES, (chunk + 1) * LANES)
+        chunks[chunk, :8] = jnp.zeros((8, LANES), F32)
+        chunks[chunk, 8:] = result[:, cut]
+        total = sum(chunks[chunk, pl.ds(s, short, stride=3), :] for s in (6, 7, 8))
+        pooled_out[:short, cut] = (total / 3.0).astype(BF16)
+    tail = (result[rows - 1 :] + result[rows - 2 : rows - 1]) / 3.0
+    extra = pooled_out.shape[0] - short
+    pooled_out[short:] = jnp.broadcast_to(tail, (extra, width)).astype(BF16)
+
+
+def short_kernel(
+    place, residual, cot, gathered, table, gain_a, w_q, w_k, w_v, w_o, gain_f, w_e, w_c, *refs
+):
+    pieces = refs[:HEADS]
+    output, grad_own, grad_all = refs[HEADS : HEADS + 3]
+    batch = (len(refs) - HEADS - 3) - 22
+    share_pieces = refs[HEADS + 3 : HEADS + 3 + batch]
+    (
+        pooled,
+        extra,
+        normed_a,
+        q_s,
+        k_s,
+        v_s,
+        o_s,
+        lse_s,
+        att,
+        middle,
+        normed_f,
+        hidden,
+        grad_pre,
+        grad_normed,
+        grad_low,
+        do_s,
+        dq_s,
+        dk_s,
+        dv_s,
+        wide,
+        share,
+        wo_s,
+    ) = refs[HEADS + 3 + batch :]
+    me, seat = place[0], place[1]
+    rows, width = residual.shape
+    count = pooled.shape[0]
+    short = rows // 3
+    full = rows * HEADS
+    chunk_count = width // LANES
+    stride = 2 * rows + short
+    ff = w_e.shape[1]
+    ff_own = ff // HEADS
+
+    for step in range(HEADS):
+        other = me ^ step
+        pooled[rows_at(other * short, short, 16), :] = pieces[step][:short].astype(F32)
+        extra[pl.ds(other, 1), :] = pieces[step][short:].astype(F32)[:1]
+    for part in range(1, HEADS):
+        at = slice(part * short, part * short + 1)
+        pooled[at] = pooled[at] + extra[part - 1 : part]
+
+    unit, _ = norm_parts(pooled[...])
+    normed_a[...] = (unit * gain_a[...]).astype(BF16)
+    low = lower_half(count)
+    turns = table[:count, :]
+    q = dot_nn(normed_a[...], w_q[...])
+    for chunk in range(chunk_count):
+        q_chunk = rope(q[:, chunk * LANES : (chunk + 1) * LANES], turns) * HEAD**-0.5
+        q_s[2 * chunk] = jnp.where(low, q_chunk, 0.0).astype(BF16)
+        q_s[2 * chunk + 1] = jnp.where(low, 0.0, q_chunk).astype(BF16)
+    k = dot_nn(normed_a[...], w_k[...])
+    for chunk in range(chunk_count):
+        k_s[chunk] = rope(k[:, chunk * LANES : (chunk + 1) * LANES], turns).astype(BF16)
+    v = dot_nn(normed_a[...], w_v[...])
+    for chunk in range(chunk_count):
+        v_s[chunk] = v[:, chunk * LANES : (chunk + 1) * LANES].astype(BF16)
+
+    low_block = lower_half(BLOCK)
+
+    def attend_chunk(chunk, carry):
+        for block in range(count // BLOCK):
+            cut = slice(block * BLOCK, (block + 1) * BLOCK)
+            seen = slice(0, (block + 1) * BLOCK)
+            results = []
+            for half in range(2):
+                scores = dot_nt(q_s[2 * chunk + half, cut, :], k_s[chunk, seen, :])
+                scores = causal(scores, block * BLOCK, 0)
+                most = jnp.max(scores, axis=-1, keepdims=True)
+                weights = jnp.exp(scores - most)
+                total = jnp.sum(weights, axis=-1, keepdims=True)
+                attended = dot_nn(weights.astype(BF16), v_s[chunk, seen, :]) / total
+                results.append((attended, most + jnp.log(total)))
+            both = jnp.where(low_block, results[0][0], results[1][0])
+            o_s[chunk, cut, :] = both
+            lse_s[chunk, cut, :] = jnp.where(low_block, results[0][1], results[1][1])
+            att[cut, rows_at(chunk * LANES, LANES, LANES)] = both.astype(BF16)
+        return carry
+
+    lax.fori_loop(0, chunk_count, attend_chunk, 0)
+    middle[...] = pooled[...] + dot_nn(att[...], w_o[...])
+    unit, scale = norm_parts(middle[...])
+    normed_f[...] = (unit * gain_f[...]).astype(BF16)
+
+    for part in range(HEADS):
+        at = part * stride + 2 * rows
+        grad_low[part * short : (part + 1) * short] = gathered[at : at + short]
+
+    ff_part = ff // 4
+    grad_normed[...] = jnp.zeros(grad_normed.shape, F32)
+
+    def feed_forward(part, carry):
+        cut = rows_at(part * ff_part, ff_part, ff_part)
+        pre = dot_nn(normed_f[...], w_e[:, cut])
+        value, slope = gelu_both(pre)
+        hidden[:, cut] = value.astype(BF16)
+        grad_hidden = dot_nt(grad_low[...], w_c[cut, :])
+        low_grad = (grad_hidden * slope).astype(BF16)
+        grad_pre[:, cut] = low_grad
+        grad_normed[...] += dot_nt(low_grad, w_e[:, cut])
+        return carry
+
+    lax.fori_loop(0, 4, feed_forward, 0)
+
+    mine = rows_at(me * short, short, 16)
+    short_out = middle[mine, :] + dot_nn(hidden[mine, :], w_c[...])
+    for chunk in range(chunk_count):
+        cut = slice(chunk * LANES, (chunk + 1) * LANES)
+        for s in range(3):
+            wide[chunk, pl.ds(s, short, stride=3), :] = short_out[:, cut]
+        output[:, cut] = residual[:, cut] + wide[chunk, :rows]
+
+    own_ff = rows_at(me * ff_own, ff_own, ff_own)
+    share[:ff_own] = dot_tn(hidden[:, own_ff], grad_low[...]).astype(BF16)
+    expand = dot_tn(normed_f[...], grad_pre[:, own_ff]).astype(BF16)
+    share[ff_own : 2 * ff_own, : width // 2] = expand[: width // 2]
+    share[ff_own : 2 * ff_own, width // 2 :] = expand[width // 2 :]
+
+    unit, scale = norm_parts(middle[...])
+    grad_middle = grad_low[...].astype(F32) + norm_back(grad_normed[...], gain_f[...], unit, scale)
+    middle[...] = grad_middle
+    g1 = grad_middle.astype(BF16)
+    d_att = dot_nt(g1, w_o[...])
+    for chunk in range(chunk_count):
+        do_chunk = d_att[:, chunk * LANES : (chunk + 1) * LANES]
+        do_s[2 * chunk] = jnp.where(low, do_chunk, 0.0).astype(BF16)
+        do_s[2 * chunk + 1] = jnp.where(low, 0.0, do_chunk).astype(BF16)
+    own_chunk = rows_at((me // 2) * LANES, LANES, LANES)
+    wo_s[...] = dot_tn(att[:, own_chunk], g1)
+
+    def attend_back(chunk, carry):
+        dk = [None] * (count // BLOCK)
+        dv = [None] * (count // BLOCK)
+        columns = rows_at(chunk * LANES, LANES, LANES)
+        for block in range(count // BLOCK):
+            cut = slice(block * BLOCK, (block + 1) * BLOCK)
+            dq = []
+            for half in range(2):
+                head = 2 * chunk + half
+                q_block, do_block = q_s[head, cut, :], do_s[head, cut, :]
+                lse = lse_s[chunk, cut, :][:, half * HEAD : half * HEAD + 1]
+                delta = jnp.sum(
+                    do_block.astype(F32) * o_s[chunk, cut, :], axis=-1, keepdims=True
+                )
+                dq_half = None
+                for key in range(block + 1):
+                    key_cut = slice(key * BLOCK, (key + 1) * BLOCK)
+                    k_block, v_block = k_s[chunk, key_cut, :], v_s[chunk, key_cut, :]
+                    scores = dot_nt(q_block, k_block)
+                    if key == block:
+                        scores = causal(scores, 0, 0)
+                    probs = jnp.exp(scores - lse)
+                    grad_probs = dot_nt(do_block, v_block)
+                    ds = (probs * (grad_probs - delta)).astype(BF16)
+                    term = dot_nn(ds, k_block)
+                    dq_half = term if dq_half is None else dq_half + term
+                    term = dot_tn(ds, q_block)
+                    dk[key] = term if dk[key] is None else dk[key] + term
+                    term = dot_tn(probs.astype(BF16), do_block)
+                    dv[key] = term if dv[key] is None else dv[key] + term
+                dq.append(dq_half)
+            both = jnp.where(low_block, dq[0], dq[1]) * HEAD**-0.5
+            dq_s[cut, columns] = rope_back(both, table[cut, :]).astype(BF16)
+        for key in range(count // BLOCK):
+            key_cut = slice(key * BLOCK, (key + 1) * BLOCK)
+            dk_s[key_cut, columns] = rope_back(dk[key], table[key_cut, :]).astype(BF16)
+            dv_s[key_cut, columns] = dv[key].astype(BF16)
+        return carry
+
+    lax.fori_loop(0, chunk_count, attend_back, 0)
+    grad_a = dot_nt(dq_s[...], w_q[...])
+    grad_a += dot_nt(dk_s[...], w_k[...])
+    grad_a += dot_nt(dv_s[...], w_v[...])
+    unit, scale = norm_parts(pooled[...])
+    grad_pooled = middle[...] + norm_back(grad_a, gain_a[...], unit, scale)
+
+    odd = me % 2 == 1
+    low_width = lower_half(width)
+    share_q = dot_tn(normed_a[...], dq_s[:, own_chunk])
+    share_k = dot_tn(normed_a[...], dk_s[:, own_chunk])
+    share_v = dot_tn(normed_a[...], dv_s[:, own_chunk])
+    share_q = jnp.where(odd, turn(share_q), share_q)
+    share_k = jnp.where(odd, share_k, turn(share_k))
+    share_v = jnp.where(odd, turn(share_v), share_v)
+    pack_attention(share, 2 * ff_own, jnp.where(low_width, share_q, share_k), fold_rows(share_v),
+                   wo_s[rows_at((me % 2) * HEAD, HEAD, HEAD), :])
+    ff_rows = 2 * ff_own // batch
+    more_rows = share_pieces[0].shape[0] - ff_rows
+    for step in range(batch):
+        peer = seat ^ step
+        share_pieces[step][:ff_rows] = share[rows_at(peer * ff_rows, ff_rows, 16), :]
+        share_pieces[step][ff_rows:] = share[
+            rows_at(2 * ff_own + peer * more_rows, more_rows, 16), :
+        ]
+
+    for chunk in range(chunk_count):
+        cut = slice(chunk * LANES, (chunk + 1) * LANES)
+        third = grad_pooled[:, cut] / 3.0
+        for s in range(3):
+            wide[chunk, pl.ds(6 + s, count, stride=3), :] = third
+        wide[chunk, full + 6 : full + 8] = jnp.zeros((2, LANES), F32)
+        grad_own[:, cut] = cot[:, cut] + wide[chunk, rows_at(me * rows + 8, rows, 8), :]
+        for part in range(HEADS):
+            at = part * stride + rows
+            more = wide[chunk, 8 + part * rows : 8 + (part + 1) * rows, :]
+            grad_all[part * rows : (part + 1) * rows, cut] = (
+                gathered[at : at + rows, cut].astype(F32) + more
+            ).astype(BF16)
+
+
+def pack_attention(share, first, both_qk, folded_v, head_rows):
+    half = both_qk.shape[0] // 2
+    share[first : first + half, :LANES] = both_qk[:half].astype(BF16)
+    share[first : first + half, LANES : 2 * LANES] = both_qk[half:].astype(BF16)
+    share[first : first + half, 2 * LANES : 3 * LANES] = folded_v.astype(BF16)
+    size = head_rows.shape[0]
+    for chunk in range(head_rows.shape[1] // LANES):
+        share[first + chunk * size : first + (chunk + 1) * size, 3 * LANES :] = head_rows[
+            :, chunk * LANES : (chunk + 1) * LANES
+        ].astype(BF16)
+
+
+def finish_back_kernel(place, grad, middle, att, normed, gain, w_o, w_e, w_c, *refs):
+    grad_middle_out, pieces, heads = refs[0], refs[1 : 1 + HEADS], refs[1 + HEADS]
+    me = place[0]
+    rows, width = grad.shape
+    _, slope = gelu_both(dot_nn(normed[...], w_e[...]))
+    grad_hidden = dot_nt(grad[...].astype(BF16), w_c[...])
+    grad_pre = (grad_hidden * slope).astype(BF16)
+    grad_normed = dot_nt(grad_pre, w_e[...])
+    unit, scale = norm_parts(middle[...])
+    grad_middle = grad[...] + norm_back(grad_normed, gain[...], unit, scale)
+    grad_middle_out[...] = grad_middle
+    g1 = grad_middle.astype(BF16)
+    d_att = dot_nt(g1, w_o[...])
+    grad_w = dot_tn(att[...], g1)
+    half = rows // 2
+    low = lower_half(half)
+    for chunk in range(width // LANES):
+        do_chunk = d_att[:, chunk * LANES : (chunk + 1) * LANES]
+        first, later = do_chunk[:half], do_chunk[half:]
+        heads[2 * chunk, :half] = jnp.where(low, first, turn(later)).astype(BF16)
+        heads[2 * chunk + 1, :half] = jnp.where(low, turn(first), later).astype(BF16)
+    for head in range(HEADS):
+        for chunk in range(width // LANES):
+            at = half + chunk * HEAD
+            heads[head, at : at + HEAD] = grad_w[
+                head * HEAD : (head + 1) * HEAD, chunk * LANES : (chunk + 1) * LANES
+            ].astype(BF16)
+    for step in range(HEADS):
+        pieces[step][...] = heads[me ^ step]
+
+
+def feed_forward_share_kernel(place, normed, grad, w_e, w_c, *refs):
+    pieces, share = refs[:-1], refs[-1]
+    seat = place[1]
+    width, ff_own = w_e.shape
+    value, slope = gelu_both(dot_nn(normed[...], w_e[...]))
+    grad_hidden = dot_nt(grad[...], w_c[...])
+    grad_pre = (grad_hidden * slope).astype(BF16)
+    share[:ff_own] = dot_tn(value.astype(BF16), grad[...]).astype(BF16)
+    expand = dot_tn(normed[...], grad_pre).astype(BF16)
+    share[ff_own:, : width // 2] = expand[: width // 2]
+    share[ff_own:, width // 2 :] = expand[width // 2 :]
+    part_rows = pieces[0].shape[0]
+    for step in range(len(pieces)):
+        pieces[step][...] = share[rows_at((seat ^ step) * part_rows, part_rows, 16), :]
+
+
+def attend_back_kernel(place, q_all, kv_all, lse_o, table, *refs):
+    pieces, outs = refs[:HEADS], refs[HEADS : 2 * HEADS]
+    dq_all, dkv_all, grad_wo, do_all, dkv_sum = refs[2 * HEADS :]
+    me = place[0]
+    rows = q_all.shape[0] // HEADS
+    half = rows // 2
+    low_half = lower_half(half)
+    total = None
+    for step in range(HEADS):
+        start = (me ^ step) * rows
+        folded = pieces[step][:half].astype(F32)
+        do_all[rows_at(start, half, 16), :] = jnp.where(low_half, 0.0, turn(folded)).astype(BF16)
+        do_all[rows_at(start + half, half, 16), :] = jnp.where(low_half, 0.0, folded).astype(BF16)
+        term = pieces[step][half:].astype(F32)
+        total = term if total is None else total + term
+    grad_wo[...] = total
+    dkv_sum[...] = jnp.zeros(dkv_sum.shape, F32)
+    for block in range(q_all.shape[0] // BLOCK):
+        cut = slice(block * BLOCK, (block + 1) * BLOCK)
+        q_block, do_block = q_all[cut], do_all[cut]
+        lse = lse_o[cut][:, :1]
+        delta = jnp.sum(do_block.astype(F32) * lse_o[cut], axis=-1, keepdims=True)
+        dq = None
+        for key in range(block + 1):
+            key_cut = slice(key * BLOCK, (key + 1) * BLOCK)
+            kv_block = kv_all[key_cut]
+            scores = dot_nt(q_block, kv_block)
+            if key == block:
+                scores = causal(scores, 0, 0)
+            probs = jnp.exp(scores - lse)
+            grad_probs = dot_nt(do_block, kv_block)
+            ds = (probs * (grad_probs - delta)).astype(BF16)
+            term = dot_nn(ds, kv_block)
+            dq = term if dq is None else dq + term
+            dkv_sum[key_cut] += dot_tn(ds, q_block) + dot_tn(probs.astype(BF16), do_block)
+        dq_all[cut] = rope_back(dq * HEAD**-0.5, table[cut, :]).astype(BF16)
+    low = lower_half(BLOCK)
+    for block in range(q_all.shape[0] // BLOCK):
+        cut = slice(block * BLOCK, (block + 1) * BLOCK)
+        dkv = dkv_sum[cut]
+        dkv_all[cut] = jnp.where(low, rope_back(dkv, table[cut, :]), dkv).astype(BF16)
+    for step in range(HEADS):
+        own = rows_at((me ^ step) * rows, rows, 16)
+        outs[step][:rows] = dkv_all[own, :]
+        outs[step][rows:] = fold_rows(dq_all[own, :].astype(F32)).astype(BF16)
+
+
+def attention_share_kernel(place, gathered, dq_all, dkv_all, grad_wo, *refs):
+    pieces, share = refs[:-1], refs[-1]
+    seat = place[1]
+    total = dq_all.shape[0]
+    rows = total // HEADS
+    stride = gathered.shape[0] // HEADS
+    width = gathered.shape[1]
+    grad_q = jnp.zeros((width, LANES), F32)
+    grad_kv = jnp.zeros((width, LANES), F32)
+    for part in range(HEADS):
+        normed = gathered[part * stride : part * stride + rows]
+        grad_q += dot_tn(normed, dq_all[part * rows : (part + 1) * rows])
+        grad_kv += dot_tn(normed, dkv_all[part * rows : (part + 1) * rows])
+    both = jnp.where(lower_half(width), grad_q, turn(grad_kv))
+    half = width // 2
+    folded_v = jnp.where(lower_half(half), turn(grad_kv[:half]), grad_kv[half:])
+    share[:half, :LANES] = both[:half].astype(BF16)
+    share[:half, LANES : 2 * LANES] = both[half:].astype(BF16)
+    share[:half, 2 * LANES : 3 * LANES] = folded_v.astype(BF16)
+    share[:half, 3 * LANES :] = grad_wo[...].astype(BF16)
+    part_rows = pieces[0].shape[0]
+    for step in range(len(pieces)):
+        pieces[step][...] = share[rows_at((seat ^ step) * part_rows, part_rows, 16), :]
+
+
+def start_back_kernel(place, x, grad_middle, gain, w_q, w_k, w_v, *refs):
+    pieces = refs[:HEADS]
+    grad_in, heads, dq, dk, dv = refs[HEADS:]
+    me = place[0]
+    rows, width = x.shape
+    half = rows // 2
+    for step in range(HEADS):
+        heads[me ^ step] = pieces[step][...]
+    low, low_half = lower_half(rows), lower_half(half)
+    for chunk in range(width // LANES):
+        cut = slice(chunk * LANES, (chunk + 1) * LANES)
+        even, odd = heads[2 * chunk].astype(F32), heads[2 * chunk + 1].astype(F32)
+        dk[:, cut] = jnp.where(low, even[:rows], turn(odd[:rows])).astype(BF16)
+        dv[:, cut] = jnp.where(low, turn(even[:rows]), odd[:rows]).astype(BF16)
+        dq[:half, cut] = jnp.where(low_half, even[rows:], turn(odd[rows:])).astype(BF16)
+        dq[half:, cut] = jnp.where(low_half, turn(even[rows:]), odd[rows:]).astype(BF16)
+    grad_a = dot_nt(dq[...], w_q[...]) + dot_nt(dk[...], w_k[...]) + dot_nt(dv[...], w_v[...])
+    unit, scale = norm_parts(x[...])
+    grad_in[...] = grad_middle[...] + norm_back(grad_a, gain[...], unit, scale)
+
+
+def column_to_row(column):
+    return jnp.transpose(jnp.broadcast_to(column, (column.shape[0], LANES)))[:1]
+
+
+def feed_forward_grads_kernel(place, gathered, w_e, gain, contract, expand, grad_gain, share, acc):
+    seat = place[1]
+    step = pl.program_id(0)
+    batch, _, width = gathered.shape[1:]
+    ff_own = w_e.shape[1]
+    part_rows = 2 * ff_own // batch
+    for peer in range(batch):
+        share[rows_at((seat ^ peer) * part_rows, part_rows, 16), :] = gathered[0, peer, :part_rows]
+    contract[...] = share[:ff_own].astype(F32)
+    half = width // 2
+    first = share[ff_own:, :half].astype(F32)
+    later = share[ff_own:, half:].astype(F32)
+    expand[:half] = first
+    expand[half:] = later
+
+    @pl.when(step == 0)
+    def _():
+        acc[...] = jnp.zeros(acc.shape, F32)
+
+    weights = w_e[...].astype(F32)
+    acc[:half] += fold_lanes(weights[:half] * first)
+    acc[half:] += fold_lanes(weights[half:] * later)
+
+    @pl.when(step == pl.num_programs(0) - 1)
+    def _():
+        total = jnp.sum(acc[...], axis=-1, keepdims=True)
+        grad_gain[...] = column_to_row(total) / gain[...]
+
+
+def fold_lanes(values):
+    return sum(
+        values[:, at : at + LANES] for at in range(0, values.shape[1], LANES)
+    )
+
+
+def attention_grads_kernel(
+    place, gathered, w_q, w_k, w_v, gain, grad_q, grad_k, grad_v, grad_o, grad_gain, share, acc
+):
+    seat = place[1]
+    step = pl.program_id(0)
+    _, batch, all_rows, width = gathered.shape
+    half = width // 2
+    part_rows = half // batch
+    for side in range(2):
+        for peer in range(batch):
+            share[side, rows_at((seat ^ peer) * part_rows, part_rows, 16), :] = gathered[
+                side, peer, all_rows - part_rows :
+            ]
+    low = lower_half(half)
+    for part in range(2):
+        rows = slice(part * half, (part + 1) * half)
+        even = share[0, :, part * LANES : (part + 1) * LANES].astype(F32)
+        odd = share[1, :, part * LANES : (part + 1) * LANES].astype(F32)
+        grad_q[rows] = jnp.where(low, even, turn(odd))
+        grad_k[rows] = jnp.where(low, turn(even), odd)
+    even = share[0, :, 2 * LANES : 3 * LANES].astype(F32)
+    odd = share[1, :, 2 * LANES : 3 * LANES].astype(F32)
+    grad_v[:half] = jnp.where(low, even, turn(odd))
+    grad_v[half:] = jnp.where(low, turn(even), odd)
+    for side in range(2):
+        for chunk in range(width // LANES):
+            grad_o[side * HEAD : (side + 1) * HEAD, chunk * LANES : (chunk + 1) * LANES] = share[
+                side, chunk * HEAD : (chunk + 1) * HEAD, 3 * LANES :
+            ].astype(F32)
+
+    @pl.when(step == 0)
+    def _():
+        acc[...] = jnp.zeros(acc.shape, F32)
+
+    acc[...] += (
+        w_q[...].astype(F32) * grad_q[...]
+        + w_k[...].astype(F32) * grad_k[...]
+        + w_v[...].astype(F32) * grad_v[...]
+    )
+
+    @pl.when(step == pl.num_programs(0) - 1)
+    def _():
+        total = jnp.sum(acc[...], axis=-1, keepdims=True)
+        grad_gain[...] = column_to_row(total) / gain[...]
+
+
+def call(kernel, out_shape, scratch, arguments, flops, limit=32):
+    specs = [pl.BlockSpec(memory_space=pltpu.SMEM)]
+    specs += [pl.BlockSpec(memory_space=pltpu.VMEM)] * (len(arguments) - 1)
+    return pl.pallas_call(
+        kernel,
+        out_shape=[jax.ShapeDtypeStruct(shape, kind) for shape, kind in out_shape],
+        in_specs=specs,
+        out_specs=[pl.BlockSpec(memory_space=pltpu.VMEM)] * len(out_shape),
+        scratch_shapes=[pltpu.VMEM(shape, kind) for shape, kind in scratch],
+        compiler_params=pltpu.CompilerParams(vmem_limit_bytes=limit * 2**20),
+        cost_estimate=pl.CostEstimate(flops=int(flops), bytes_accessed=2**20, transcendentals=0),
+    )(*arguments)
+
+
+def exchange(pieces, axis):
+    devices = range(lax.axis_size(axis))
+    moved = {
+        step: lax.ppermute(pieces[step], axis, [(i, i ^ step) for i in devices])
+        for step in reversed(range(1, len(pieces)))
+    }
+    return [pieces[0]] + [moved[step] for step in range(1, len(pieces))]
+
+
+def sum_over_batch(pieces):
+    arrived = exchange(pieces, "batch")
+    total = sum(piece.astype(F32) for piece in arrived).astype(BF16)
+    return jnp.stack(exchange([total] * len(pieces), "batch"))
+
+
+def gather(block):
+    return lax.all_gather(block, "seq", axis=0, tiled=True)
+
+
+def feed_forward_grads(place, gathered, params):
+    parts, batch, rows, width = gathered.shape
+    ff = params[6].shape[1]
+    ff_own = ff // parts
+    return pl.pallas_call(
+        feed_forward_grads_kernel,
+        grid_spec=pltpu.PrefetchScalarGridSpec(
+            num_scalar_prefetch=1,
+            grid=(parts,),
+            in_specs=[
+                pl.BlockSpec((1, batch, rows, width), lambda i, s: (i, 0, 0, 0)),
+                pl.BlockSpec((width, ff_own), lambda i, s: (0, i)),
+                pl.BlockSpec((1, width), lambda i, s: (0, 0)),
+            ],
+            out_specs=[
+                pl.BlockSpec((ff_own, width), lambda i, s: (i, 0)),
+                pl.BlockSpec((width, ff_own), lambda i, s: (0, i)),
+                pl.BlockSpec((1, width), lambda i, s: (0, 0)),
+            ],
+            scratch_shapes=[
+                pltpu.VMEM((2 * ff_own, width), BF16),
+                pltpu.VMEM((width, LANES), F32),
+            ],
+        ),
+        out_shape=[
+            jax.ShapeDtypeStruct((ff, width), F32),
+            jax.ShapeDtypeStruct((width, ff), F32),
+            jax.ShapeDtypeStruct((1, width), F32),
+        ],
+        cost_estimate=pl.CostEstimate(flops=10**9, bytes_accessed=2**23, transcendentals=0),
+    )(place, gathered, params[6], params[5])
+
+
+def attention_grads(place, gathered, params):
+    parts, batch, rows, width = gathered.shape
+    column = pl.BlockSpec((width, LANES), lambda i, s: (0, i))
+    row = pl.BlockSpec((1, width), lambda i, s: (0, 0))
+    square = jax.ShapeDtypeStruct((width, width), F32)
+    return pl.pallas_call(
+        attention_grads_kernel,
+        grid_spec=pltpu.PrefetchScalarGridSpec(
+            num_scalar_prefetch=1,
+            grid=(parts // 2,),
+            in_specs=[
+                pl.BlockSpec((2, batch, rows, width), lambda i, s: (i, 0, 0, 0)),
+                column,
+                column,
+                column,
+                row,
+            ],
+            out_specs=[
+                column,
+                column,
+                column,
+                pl.BlockSpec((LANES, width), lambda i, s: (i, 0)),
+                row,
+            ],
+            scratch_shapes=[
+                pltpu.VMEM((2, width // 2, width), BF16),
+                pltpu.VMEM((width, LANES), F32),
+            ],
+        ),
+        out_shape=[square, square, square, square, jax.ShapeDtypeStruct((1, width), F32)],
+        cost_estimate=pl.CostEstimate(flops=10**9, bytes_accessed=2**22, transcendentals=0),
+    )(place, gathered, params[1], params[2], params[3], params[0])
+
+
+def by_heads(inputs, cotangent, *weights):
+    full = (weights[0][None],) + weights[1:5] + (weights[5][None],) + weights[6:8]
+    brief = (weights[8][None],) + weights[9:13] + (weights[13][None],) + weights[14:16]
+    x, cot = inputs[0], cotangent[0]
+    rows, width = x.shape
+    short, half, total = rows // 3, rows // 2, rows * HEADS
+    batch = lax.axis_size("batch")
+    ff = full[6].shape[1]
+    ff_own = ff // HEADS
+    count = short * HEADS
+    chunks = width // LANES
+    unit = 2.0 * rows * width * width
+    place = jnp.stack([lax.axis_index("seq"), lax.axis_index("batch")]).astype(jnp.int32)
+    table = rope_constants(total)
+    block = rows + half
+
+    outs = call(
+        project_kernel,
+        [((block, LANES), BF16)] * HEADS + [((2 * rows + short, width), BF16)],
+        [((HEADS, block, LANES), BF16), ((chunks, rows, LANES), F32)],
+        (place, x, cot, full[0], full[1], full[2], full[3], table),
+        3 * unit,
+    )
+    pieces, bundle = exchange(outs[:HEADS], "seq"), outs[HEADS]
+    gathered = gather(bundle)
+
+    outs = call(
+        attend_kernel,
+        [((half, LANES), BF16)] * HEADS
+        + [((total, LANES), BF16), ((total, LANES), BF16), ((total, LANES), F32)],
+        [],
+        (place, *pieces),
+        12 * unit,
+    )
+    pieces = exchange(outs[:HEADS], "seq")
+    q_all, kv_all, lse_o = outs[HEADS:]
+
+    residual, middle, att, normed_f, pooled = call(
+        finish_kernel,
+        [
+            ((rows, width), F32),
+            ((rows, width), F32),
+            ((rows, width), BF16),
+            ((rows, width), BF16),
+            ((short + 16, width), BF16),
+        ],
+        [((HEADS, half, LANES), F32), ((chunks, rows + 8, LANES), F32)],
+        (place, x, full[5], full[4], full[6], full[7], *pieces),
+        9 * unit,
+    )
+    pieces = exchange([pooled] * HEADS, "seq")
+    normed_all = gather(normed_f)
+
+    part_rows = (2 * ff_own + width // 2) // batch
+    outs = call(
+        short_kernel,
+        [((rows, width), F32), ((rows, width), F32), ((total, width), BF16)]
+        + [((part_rows, width), BF16)] * batch,
+        [
+            ((count, width), F32),
+            ((HEADS, width), F32),
+            ((count, width), BF16),
+            ((HEADS, count, LANES), BF16),
+            ((chunks, count, LANES), BF16),
+            ((chunks, count, LANES), BF16),
+            ((chunks, count, LANES), F32),
+            ((chunks, count, LANES), F32),
+            ((count, width), BF16),
+            ((count, width), F32),
+            ((count, width), BF16),
+            ((count, ff), BF16),
+            ((count, ff), BF16),
+            ((count, width), F32),
+            ((count, width), BF16),
+            ((HEADS, count, LANES), BF16),
+            ((count, width), BF16),
+            ((count, width), BF16),
+            ((count, width), BF16),
+            ((chunks, total + 16, LANES), F32),
+            ((2 * ff_own + width // 2, width), BF16),
+            ((LANES, width), F32),
+        ],
+        (place, residual, cot, gathered, table) + brief + tuple(pieces),
+        60 * unit,
+        60,
+    )
+    output, grad_own, grad_all = outs[:3]
+    short_share = gather(sum_over_batch(outs[3:])[None])
+
+    outs = call(
+        finish_back_kernel,
+        [((rows, width), F32)] + [((half + 4 * HEAD, LANES), BF16)] * HEADS,
+        [((HEADS, half + 4 * HEAD, LANES), BF16)],
+        (place, grad_own, middle, att, normed_f, full[5], full[4], full[6], full[7]),
+        14 * unit,
+    )
+    grad_middle = outs[0]
+    pieces = exchange(outs[1:], "seq")
+
+    whole = pl.BlockSpec((total, width), lambda i, s: (0, 0))
+    piece = pl.BlockSpec((2 * ff_own // batch, width), lambda i, s: (0, 0))
+    outs = pl.pallas_call(
+        feed_forward_share_kernel,
+        grid_spec=pltpu.PrefetchScalarGridSpec(
+            num_scalar_prefetch=1,
+            grid=(1,),
+            in_specs=[
+                whole,
+                whole,
+                pl.BlockSpec((width, ff_own), lambda i, s: (0, s[0])),
+                pl.BlockSpec((ff_own, width), lambda i, s: (s[0], 0)),
+            ],
+            out_specs=[piece] * batch,
+            scratch_shapes=[pltpu.VMEM((2 * ff_own, width), BF16)],
+        ),
+        out_shape=[jax.ShapeDtypeStruct((2 * ff_own // batch, width), BF16)] * batch,
+        compiler_params=pltpu.CompilerParams(vmem_limit_bytes=32 * 2**20),
+        cost_estimate=pl.CostEstimate(
+            flops=int(20 * unit), bytes_accessed=2**22, transcendentals=0
+        ),
+    )(place, normed_all, grad_all, full[6], full[7])
+    ff_share = gather(sum_over_batch(outs)[None])
+
+    outs = call(
+        attend_back_kernel,
+        [((block, LANES), BF16)] * HEADS
+        + [((total, LANES), BF16), ((total, LANES), BF16), ((4 * HEAD, LANES), F32)],
+        [((total, LANES), BF16), ((total, LANES), F32)],
+        (place, q_all, kv_all, lse_o, table, *pieces),
+        20 * unit,
+    )
+    pieces = exchange(outs[:HEADS], "seq")
+    dq_all, dkv_all, grad_wo = outs[HEADS:]
+    outs = call(
+        attention_share_kernel,
+        [((width // 2 // batch, width), BF16)] * batch,
+        [((width // 2, width), BF16)],
+        (place, gathered, dq_all, dkv_all, grad_wo),
+        8 * unit,
+    )
+    attention_share = gather(sum_over_batch(outs)[None])
+
+    (grad_in,) = call(
+        start_back_kernel,
+        [((rows, width), F32)],
+        [((HEADS, block, LANES), BF16)] + [((rows, width), BF16)] * 3,
+        (place, x, grad_middle, full[0], full[1], full[2], full[3], *pieces),
+        6 * unit,
+    )
+
+    def arranged(attention, feed_forward):
+        grad_q, grad_k, grad_v, grad_o, grad_gain_a = attention
+        contract, expand, grad_gain_f = feed_forward
+        return (grad_gain_a[0], grad_q, grad_k, grad_v, grad_o, grad_gain_f[0], expand, contract)
+
+    short_grads = arranged(
+        attention_grads(place, short_share, brief), feed_forward_grads(place, short_share, brief)
+    )
+    full_grads = arranged(
+        attention_grads(place, attention_share, full), feed_forward_grads(place, ff_share, full)
+    )
+    return (output[None], grad_in[None]) + full_grads + short_grads
 
 
 def from_behind(block, axis, distance):
@@ -336,7 +1254,7 @@
     )
 
 
-def local(
+def by_rows(
     inputs,
     cotangent,
     full_gain_attn,
@@ -533,44 +1451,13 @@
 
 
 def solution(mesh):
-    in_specs = (
-        P("batch", "seq", None),
-        P("batch", "seq", None),
-        P(),
-        P(),
-        P(),
-        P(),
-        P(),
-        P(),
-        P(),
-        P(),
-        P(),
-        P(),
-        P(),
-        P(),
-        P(),
-        P(),
-        P(),
-        P(),
-    )
-    out_specs = (
-        P("batch", "seq", None),
-        P("batch", "seq", None),
-        P(),
-        P(),
-        P(),
-        P(),
-        P(),
-        P(),
-        P(),
-        P(),
-        P(),
-        P(),
-        P(),
-        P(),
-        P(),
-        P(),
-        P(),
-        P(),
-    )
-    return jax.shard_map(local, mesh=mesh, in_specs=in_specs, out_specs=out_specs, check_vma=False)
+    sequence = P("batch", "seq", None)
+    seq, batch = mesh.shape["seq"], mesh.shape["batch"]
+    fits = seq == HEADS and batch & (batch - 1) == 0
+    return jax.shard_map(
+        by_heads if fits else by_rows,
+        mesh=mesh,
+        in_specs=(sequence, sequence) + (P(),) * 16,
+        out_specs=(sequence, sequence) + (P(),) * 16,
+        check_vma=False,
+    )

time: 758 us -> 286 us (0.38); the launches traced: 748 us -> 285 us
  waiting for transfers between devices: 409 us -> 90.7 us
  blocking collectives: 117 us -> 0 us
  matrix products: 103 us -> 0 us
  Pallas kernels: 0 us -> 93.5 us
  starting transfers between devices: 4.84 us -> 64.9 us
  other arithmetic: 61.8 us -> 2.87 us
  local copies, waits for them, and re-layouts: 35.2 us -> 18.8 us
    reduce_scatter x6 -> x0, waiting for transfers between devices: 220 us -> none  [the longest x1 45.5 us: local(): lax.psum_scatter(full_grads[6].astype(jnp.bfloat16), 'seq', scatter_dimen...]
    dot_general x48 -> x0, matrix products: 103 us -> none  [the longest x2 10.5 us: finish_back(): jnp.einsum('nd,fd->nf', grad_low, params[7], preferred_element_type=jnp.f...]
    pallas_call x0 -> x13, Pallas kernels: none -> 93.5 us  [the longest x8 58.1 us: call(): pl.pallas_call(kernel, out_shape=[jax.ShapeDtypeStruct(shape, kind) for s...]
    all_gather x8 -> x0, blocking collectives: 81.3 us -> none  [the longest x1 11.4 us: local(): lax.all_gather(totals[2].astype(jnp.bfloat16), 'seq', axis=0, tiled=True)]
    psum x1 -> x0, waiting for transfers between devices: 77.6 us -> none  [local(): lax.psum(shares[1].astype(jnp.bfloat16), 'batch').astype(jnp.float32)]
    ppermute x2 -> x53, waiting for transfers between devices: 2.35 us -> 75.9 us  [exchange(): lax.ppermute(pieces[step], axis, [(i, i ^ step) for i in devices])]
    ppermute x2 -> x53, starting transfers between devices: 3.77 us -> 64.5 us  [exchange(): lax.ppermute(pieces[step], axis, [(i, i ^ step) for i in devices])]
    all_gather x8 -> x5, waiting for transfers between devices: 72.4 us -> 14.7 us  [gather(): return lax.all_gather(block, 'seq', axis=0, tiled=True)]
  transfers between devices with their start and end apart: 18 -> 58, of which waited for: 14 -> 30; matrix products, arithmetic and copies ran while one was open for 14% -> 1% of each run, Pallas kernels for 0% -> 26%
where the time goes in v1:
time: 286 us; the launch traced here: 285 us
  Pallas kernels  93.5 us (33%)
  waiting for transfers between devices  90.7 us (32%)
  starting transfers between devices  64.9 us (23%)
  local copies, waits for them, and re-layouts  18.8 us (7%)
  between operations  14.4 us (5%)
  other arithmetic  2.87 us (1%)
    ppermute x53, waiting for transfers between devices, exchange(): lax.ppermute(pieces[step], axis, [(i, i ^ step) for i in devices])  75.9 us
    ppermute x53, starting transfers between devices, exchange(): lax.ppermute(pieces[step], axis, [(i, i ^ step) for i in devices])  64.5 us
    pallas_call x8, Pallas kernels, call(): pl.pallas_call(kernel, out_shape=[jax.ShapeDtypeStruct(shape, kind) for s...  58.1 us
    pallas_call x2, Pallas kernels, feed_forward_grads(): pl.pallas_call(feed_forward_grads_kernel, grid_spec=pltpu.PrefetchScalarG...  19.3 us
    unnamed x114, local copies, waits for them, and re-layouts  18.8 us
    all_gather x5, waiting for transfers between devices, gather(): return lax.all_gather(block, 'seq', axis=0, tiled=True)  14.7 us
    pallas_call x2, Pallas kernels, attention_grads(): pl.pallas_call(attention_grads_kernel, grid_spec=pltpu.PrefetchScalarGrid...  13.1 us
  transfers between devices with their start and end apart: 58, of which 30 were waited for; matrix products, arithmetic and copies ran while one was open for 1% of the time, Pallas kernels for 26%

profile of v1, /device:TPU:0, one launch (start us, length us, event | category | flops | bytes accessed | tf_op | source)
XLA Modules:
  0.0 285.1 jit_solution(4367625226033999296)
XLA Ops:
  14.5 2.4 shard_map.322
  17.5 2.6 collective-permute-start.1
  21.9 2.6 collective-permute-start.5
  24.9 4.0 %collective-permute-done.4.refs_5_ = bf16[288,128]{1,0:T(8,128)(2,1)S(1)} collective-permute-done((bf16[288,128]{1,0:T(8,128)(2,1)S(1)}, bf16[288,128]{1,0:T(8,128)(2,1)S(1)}, u32[]{:S(2)}, u32[]{:S(2)}) %collective-permute-start.4) | collective-permute-done | bytes 73760 | tf_op jit(solution)/shard_map/ppermute | solution.py:686
  29.7 3.8 %shard_map.323 = (bf16[96,128]{1,0:T(8,128)(2,1)S(1)}, bf16[96,128]{1,0:T(8,128)(2,1)S(1)}, bf16[96,128]{1,0:T(8,128)(2,1)S(1)}, bf16[96,128]{1,0:T(8,128)(2,1)S...) custom-call(s32[2]{0:T(128)S(1)} %pad_add_fusion.place, ...), custom_call_target="tpu_custom_call" | custom-call | flops 1207959552 | bytes 1048576 | tf_op jit(solution)/shard_map/pallas_call | solution.py:672
  37.7 2.4 collective-permute-start.12
  44.6 2.8 shard_map.324
  62.7 32.8 %shard_map.325 = (f32[192,512]{1,0:T(8,128)}, f32[192,512]{1,0:T(8,128)}, bf16[1536,512]{1,0:T(8,128)(2,1)}, bf16[192,512]{1,0:T(8,128)(2,1)}, bf16[192,512]{1,0...) custom-call(s32[2]{0:T(128)} %copy-done.22, f32[192,512]{1,0:T(8,128)} %copy-done.28, ...), custom_call_target="tpu_custom_call" | custom-call | flops 6039797760 | bytes 1048576 | tf_op jit(solution)/shard_map/pallas_call | solution.py:672
  99.0 3.9 %shard_map.326 = (f32[192,512]{1,0:T(8,128)S(1)}, bf16[352,128]{1,0:T(8,128)(2,1)S(1)}, bf16[352,128]{1,0:T(8,128)(2,1)S(1)}, bf16[352,128]{1,0:T(8,128)(2,1)S(1...) custom-call(s32[2]{0:T(128)S(1)} %copy-done.23, ...), custom_call_target="tpu_custom_call" | custom-call | flops 1409286144 | bytes 1048576 | tf_op jit(solution)/shard_map/pallas_call | solution.py:672
  110.3 4.6 %collective-permute-done.25.refs_5_ = bf16[352,128]{1,0:T(8,128)(2,1)S(1)} collective-permute-done((bf16[352,128]{1,0:T(8,128)(2,1)S(1)}, bf16[352,128]{1,0:T(8,128)(2,1)S(1)}, u32[]{:S(2)}, u32[]{:S(2)}) %collective-permute-start.25) | collective-permute-done | bytes 90144 | tf_op jit(solution)/shard_map/ppermute | solution.py:686
  114.9 8.1 %shard_map.327 = (bf16[288,128]{1,0:T(8,128)(2,1)S(1)}, bf16[288,128]{1,0:T(8,128)(2,1)S(1)}, bf16[288,128]{1,0:T(8,128)(2,1)S(1)}, bf16[288,128]{1,0:T(8,128)(2...) custom-call(s32[2]{0:T(128)S(1)} %copy-done.23, ...), custom_call_target="tpu_custom_call" | custom-call | flops 2013265920 | bytes 1048576 | tf_op jit(solution)/shard_map/pallas_call | solution.py:672
  123.1 2.2 shard_map.329
  127.3 2.5 collective-permute-start.36
  130.0 5.0 %collective-permute-done.36 = bf16[64,512]{1,0:T(8,128)(2,1)S(1)} collective-permute-done((bf16[64,512]{1,0:T(8,128)(2,1)S(1)}, bf16[64,512]{1,0:T(8,128)(2,1)S(1)}, u32[]{:S(2)}, u32[]{:S(2)}) %collective-permute-start.36) | collective-permute-done | bytes 65568 | tf_op jit(solution)/shard_map/ppermute | solution.py:686
  136.0 2.4 collective-permute-start.40
  149.9 3.0 %shard_map.331 = (bf16[128,512]{1,0:T(8,128)(2,1)S(1)}, bf16[128,512]{1,0:T(8,128)(2,1)S(1)}, bf16[128,512]{1,0:T(8,128)(2,1)S(1)}, bf16[128,512]{1,0:T(8,128)(2,1)S(1)}) custom-call(s32[2]{0:T(128)S(1)} %copy-done.23, bf16[1536,512]{1,0:T(8,128)(2,1)S(1)} %copy-done.27, bf16[1536,512]{1,0:T(8,128)(2,1)S(1)} %copy-done.42, bf16[512,2048]{1,0:T(8,128)(2,1)S(1)} %copy-done, ...), custom_call_target="tpu_custom_call" | custom-call | flops 2013265920 | bytes 4194304 | tf_op jit(solution)/shard_map/pallas_call | solution.py:870
  155.2 2.2 collective-permute-start.43
  157.4 2.3 collective-permute-done.41
  159.7 6.1 %collective-permute-done.42 = bf16[128,512]{1,0:T(8,128)(2,1)S(1)} collective-permute-done((bf16[128,512]{1,0:T(8,128)(2,1)S(1)}, bf16[128,512]{1,0:T(8,128)(2,1)S(1)}, u32[]{:S(2)}, u32[]{:S(2)}) %collective-permute-start.42) | collective-permute-done | bytes 131104 | tf_op jit(solution)/shard_map/ppermute | solution.py:686
  170.3 3.7 %collective-permute-done.46 = bf16[128,512]{1,0:T(8,128)(2,1)S(1)} collective-permute-done((bf16[128,512]{1,0:T(8,128)(2,1)S(1)}, bf16[128,512]{1,0:T(8,128)(2,1)S(1)}, u32[]{:S(2)}, u32[]{:S(2)}) %collective-permute-start.46) | collective-permute-done | bytes 131104 | tf_op jit(solution)/shard_map/ppermute | solution.py:686
  174.1 4.6 %collective-permute-done.45 = bf16[128,512]{1,0:T(8,128)(2,1)S(1)} collective-permute-done((bf16[128,512]{1,0:T(8,128)(2,1)S(1)}, bf16[128,512]{1,0:T(8,128)(2,1)S(1)}, u32[]{:S(2)}, u32[]{:S(2)}) %collective-permute-start.45) | collective-permute-done | bytes 131104 | tf_op jit(solution)/shard_map/ppermute | solution.py:686
  181.5 2.6 collective-permute-start.49
  184.1 4.0 %collective-permute-done.47 = bf16[192,512]{1,0:T(8,128)(2,1)S(1)} collective-permute-done((bf16[192,512]{1,0:T(8,128)(2,1)}, bf16[192,512]{1,0:T(8,128)(2,1)S(1)}, u32[]{:S(2)}, u32[]{:S(2)}) %collective-permute-start.47) | collective-permute-done | bytes 196640 | tf_op jit(solution)/shard_map/ppermute | solution.py:686
  188.2 8.6 %collective-permute-done.48 = bf16[192,512]{1,0:T(8,128)(2,1)S(1)} collective-permute-done((bf16[192,512]{1,0:T(8,128)(2,1)}, bf16[192,512]{1,0:T(8,128)(2,1)S(1)}, u32[]{:S(2)}, u32[]{:S(2)}) %collective-permute-start.48) | collective-permute-done | bytes 196640 | tf_op jit(solution)/shard_map/ppermute | solution.py:686
  198.8 9.8 %collective-permute-start.51 = (bf16[192,512]{1,0:T(8,128)(2,1)S(1)}, bf16[192,512]{1,0:T(8,128)(2,1)S(1)}, u32[]{:S(2)}, u32[]{:S(2)}) collective-permute-start(bf16[192,512]{1,0:T(8,128)(2,1)S(1)} %add_convert_fusion), channel_id=1, source_target_pairs={{0,16},{8,24},{16,0},{24,8},{1,17},{9,25},{17,1},{25,9},{2,18},{10... | collective-permute-start | bytes 589832 | tf_op jit(solution)/shard_map/ppermute | solution.py:686
  208.6 7.8 %collective-permute-done.51 = bf16[192,512]{1,0:T(8,128)(2,1)S(1)} collective-permute-done((bf16[192,512]{1,0:T(8,128)(2,1)S(1)}, bf16[192,512]{1,0:T(8,128)(2,1)S(1)}, u32[]{:S(2)}, u32[]{:S(2)}) %collective-permute-start.51) | collective-permute-done | bytes 196640 | tf_op jit(solution)/shard_map/ppermute | solution.py:686
  224.5 2.6 collective-permute-done.32.refs_5_
  231.5 5.9 %shard_map.330 = (f32[512,512]{1,0:T(8,128)}, f32[512,512]{1,0:T(8,128)}, f32[512,512]{1,0:T(8,128)}, f32[512,512]{1,0:T(8,128)}, f32[1,512]{1,0:T(1,128)}) custom-call(s32[2]{0:T(128)} %copy-done.22, bf16[8,4,64,512]{3,2,1,0:T(8,128)(2,1)} %bitcast.60, bf16[512,512]{1,0:T(8,128)(2,1)} %w_q.8, bf16[512,512]{1,0:T(8,128)(2,1)} %w_k.8, bf16[512,512]{1,0:T(8,128)(2,1)} %w_v.8, ...), custom_call_target="tpu_custom_call" | custom-call | flops 1000000000 | bytes 4194304 | tf_op jit(solution)/shard_map/pallas_call | solution.py:740
  237.4 9.2 %shard_map.332 = (f32[2048,512]{1,0:T(8,128)}, f32[512,2048]{1,0:T(8,128)}, f32[1,512]{1,0:T(1,128)}) custom-call(s32[2]{0:T(128)} %copy-done.22, bf16[8,4,128,512]{3,2,1,0:T(8,128)(2,1)} %bitcast.42, bf16[512,2048]{1,0:T(8,128)(2,1)} %w_e.10, f32[1,512]{1,0:T(1,128)} %bitcast.34), custom_call_target="tpu_custom_call" | custom-call | flops 1000000000 | bytes 8388608 | tf_op jit(solution)/shard_map/pallas_call | solution.py:706
  246.7 14.7 %all-gather.17.cloned.1.call-done = bf16[32,192,512]{2,1,0:T(8,128)(2,1)} async-done(((bf16[4,192,512]{2,1,0:T(8,128)(2,1)}), bf16[32,192,512]{2,1,0:T(8,128)(2,1)}) %all-gather.17.cloned.1.call-update) | async-done | bytes 6291472 | tf_op jit(solution)/shard_map/all_gather | solution.py:699
  261.3 7.2 %shard_map.333 = (f32[512,512]{1,0:T(8,128)}, f32[512,512]{1,0:T(8,128)}, f32[512,512]{1,0:T(8,128)}, f32[512,512]{1,0:T(8,128)}, f32[1,512]{1,0:T(1,128)}) custom-call(s32[2]{0:T(128)} %copy-done.22, bf16[8,4,192,512]{3,2,1,0:T(8,128)(2,1)} %bitcast.40, bf16[512,512]{1,0:T(8,128)(2,1)} %w_q.9, bf16[512,512]{1,0:T(8,128)(2,1)} %w_k.9, bf16[512,512]{1,0:T(8,128)(2,1)} %w_v.9, ...), custom_call_target="tpu_custom_call" | custom-call | flops 1000000000 | bytes 4194304 | tf_op jit(solution)/shard_map/pallas_call | solution.py:740
  268.5 10.1 %shard_map.334 = (f32[2048,512]{1,0:T(8,128)}, f32[512,2048]{1,0:T(8,128)}, f32[1,512]{1,0:T(1,128)}) custom-call(s32[2]{0:T(128)} %copy-done.22, bf16[8,4,192,512]{3,2,1,0:T(8,128)(2,1)} %bitcast.41, bf16[512,2048]{1,0:T(8,128)(2,1)} %w_e.11, f32[1,512]{1,0:T(1,128)} %bitcast.59), custom_call_target="tpu_custom_call" | custom-call | flops 1000000000 | bytes 8388608 | tf_op jit(solution)/shard_map/pallas_call | solution.py:706
  (223 shorter events, 84.1 us)
Async XLA Ops:
  7.2 55.4 %all-gather.9.cloned.1.call-start = ((), (), s32[]{:S(2)}) async-start(), calls=%async_computation | async-start | bytes 4128768 | tf_op jit(solution)/shard_map/all_gather | solution.py:699
  16.9 128.5 %all-gather.11.cloned.1.call-start = ((), (), s32[]{:S(2)}) async-start(), calls=%async_computation.1 | async-start | bytes 1769472 | tf_op jit(solution)/shard_map/all_gather | solution.py:699
  17.5 7.0 %collective-permute-start.1 = (bf16[288,128]{1,0:T(8,128)(2,1)S(1)}, bf16[288,128]{1,0:T(8,128)(2,1)S(1)}, u32[]{:S(2)}, u32[]{:S(2)}) collective-permute-start(bf16[288,128]{1,0:T(8,128)(2,1)S(1)} %get-tuple-element.96), channel_id=1, source_target_pairs={{0,2},{1,3},{2,0},{3,1},{4,6},{5,7},{6,4},{7,5},{8,10},{9,11},{10,... | collective-permute-start | bytes 221192 | tf_op jit(solution)/shard_map/ppermute | solution.py:686
  21.9 7.0 %collective-permute-start.4 = (bf16[288,128]{1,0:T(8,128)(2,1)S(1)}, bf16[288,128]{1,0:T(8,128)(2,1)S(1)}, u32[]{:S(2)}, u32[]{:S(2)}) collective-permute-start(bf16[288,128]{1,0:T(8,128)(2,1)S(1)} %get-tuple-element.99), channel_id=1, source_target_pairs={{0,5},{1,4},{2,7},{3,6},{4,1},{5,0},{6,3},{7,2},{8,13},{9,12},{10,... | collective-permute-start | bytes 221192 | tf_op jit(solution)/shard_map/ppermute | solution.py:686
  21.9 7.0 %collective-permute-start.5 = (bf16[288,128]{1,0:T(8,128)(2,1)S(1)}, bf16[288,128]{1,0:T(8,128)(2,1)S(1)}, u32[]{:S(2)}, u32[]{:S(2)}) collective-permute-start(bf16[288,128]{1,0:T(8,128)(2,1)S(1)} %get-tuple-element.100), channel_id=1, source_target_pairs={{0,6},{1,7},{2,4},{3,5},{4,2},{5,3},{6,0},{7,1},{8,14},{9,15},{10,... | collective-permute-start | bytes 221192 | tf_op jit(solution)/shard_map/ppermute | solution.py:686
  33.8 6.3 %collective-permute-start.8 = (bf16[96,128]{1,0:T(8,128)(2,1)S(1)}, bf16[96,128]{1,0:T(8,128)(2,1)S(1)}, u32[]{:S(2)}, u32[]{:S(2)}) collective-permute-start(bf16[96,128]{1,0:T(8,128)(2,1)S(1)} %get-tuple-element.104), channel_id=1, source_target_pairs={{0,2},{1,3},{2,0},{3,1},{4,6},{5,7},{6,4},{7,5},{8,10},{9,11},{10,... | collective-permute-start | bytes 73736 | tf_op jit(solution)/shard_map/ppermute | solution.py:686
  49.6 181.9 %all-gather.13.cloned.1.call-start = ((), (), s32[]{:S(2)}) async-start(), calls=%async_computation.2 | async-start | bytes 2359296 | tf_op jit(solution)/shard_map/all_gather | solution.py:699
  51.1 6.8 %collective-permute-start.19 = (bf16[80,512]{1,0:T(8,128)(2,1)S(1)}, bf16[80,512]{1,0:T(8,128)(2,1)S(1)}, u32[]{:S(2)}, u32[]{:S(2)}) collective-permute-start(bf16[80,512]{1,0:T(8,128)(2,1)S(1)} %get-tuple-element.112.refs_0_), channel_id=1, source_target_pairs={{0,6},{1,7},{2,4},{3,5},{4,2},{5,3},{6,0},{7,1},{8,14},{9,15},{10,... | collective-permute-start | bytes 245768 | tf_op jit(solution)/shard_map/ppermute | solution.py:686
  52.4 7.1 %collective-permute-start.18 = (bf16[80,512]{1,0:T(8,128)(2,1)S(1)}, bf16[80,512]{1,0:T(8,128)(2,1)S(1)}, u32[]{:S(2)}, u32[]{:S(2)}) collective-permute-start(bf16[80,512]{1,0:T(8,128)(2,1)S(1)} %get-tuple-element.112.refs_0_), channel_id=1, source_target_pairs={{0,5},{1,4},{2,7},{3,6},{4,1},{5,0},{6,3},{7,2},{8,13},{9,12},{10,... | collective-permute-start | bytes 245768 | tf_op jit(solution)/shard_map/ppermute | solution.py:686
  52.5 8.8 %collective-permute-start.17 = (bf16[80,512]{1,0:T(8,128)(2,1)S(1)}, bf16[80,512]{1,0:T(8,128)(2,1)S(1)}, u32[]{:S(2)}, u32[]{:S(2)}) collective-permute-start(bf16[80,512]{1,0:T(8,128)(2,1)S(1)} %get-tuple-element.112.refs_0_), channel_id=1, source_target_pairs={{0,4},{1,5},{2,6},{3,7},{4,0},{5,1},{6,2},{7,3},{8,12},{9,13},{10,... | collective-permute-start | bytes 245768 | tf_op jit(solution)/shard_map/ppermute | solution.py:686
  54.3 7.0 %collective-permute-start.16 = (bf16[80,512]{1,0:T(8,128)(2,1)S(1)}, bf16[80,512]{1,0:T(8,128)(2,1)S(1)}, u32[]{:S(2)}, u32[]{:S(2)}) collective-permute-start(bf16[80,512]{1,0:T(8,128)(2,1)S(1)} %get-tuple-element.112.refs_0_), channel_id=1, source_target_pairs={{0,3},{1,2},{2,1},{3,0},{4,7},{5,6},{6,5},{7,4},{8,11},{9,10},{10,... | collective-permute-start | bytes 245768 | tf_op jit(solution)/shard_map/ppermute | solution.py:686
  105.1 9.8 %collective-permute-start.25 = (bf16[352,128]{1,0:T(8,128)(2,1)S(1)}, bf16[352,128]{1,0:T(8,128)(2,1)S(1)}, u32[]{:S(2)}, u32[]{:S(2)}) collective-permute-start(bf16[352,128]{1,0:T(8,128)(2,1)S(1)} %get-tuple-element.127), channel_id=1, source_target_pairs={{0,5},{1,4},{2,7},{3,6},{4,1},{5,0},{6,3},{7,2},{8,13},{9,12},{10,... | collective-permute-start | bytes 270344 | tf_op jit(solution)/shard_map/ppermute | solution.py:686
  106.5 8.4 %collective-permute-start.26 = (bf16[352,128]{1,0:T(8,128)(2,1)S(1)}, bf16[352,128]{1,0:T(8,128)(2,1)S(1)}, u32[]{:S(2)}, u32[]{:S(2)}) collective-permute-start(bf16[352,128]{1,0:T(8,128)(2,1)S(1)} %get-tuple-element.128), channel_id=1, source_target_pairs={{0,6},{1,7},{2,4},{3,5},{4,2},{5,3},{6,0},{7,1},{8,14},{9,15},{10,... | collective-permute-start | bytes 270344 | tf_op jit(solution)/shard_map/ppermute | solution.py:686
  108.4 6.5 %collective-permute-start.27 = (bf16[352,128]{1,0:T(8,128)(2,1)S(1)}, bf16[352,128]{1,0:T(8,128)(2,1)S(1)}, u32[]{:S(2)}, u32[]{:S(2)}) collective-permute-start(bf16[352,128]{1,0:T(8,128)(2,1)S(1)} %get-tuple-element.129), channel_id=1, source_target_pairs={{0,7},{1,6},{2,5},{3,4},{4,3},{5,2},{6,1},{7,0},{8,15},{9,14},{10,... | collective-permute-start | bytes 270344 | tf_op jit(solution)/shard_map/ppermute | solution.py:686
  127.3 7.7 %collective-permute-start.36 = (bf16[64,512]{1,0:T(8,128)(2,1)S(1)}, bf16[64,512]{1,0:T(8,128)(2,1)S(1)}, u32[]{:S(2)}, u32[]{:S(2)}) collective-permute-start(bf16[64,512]{1,0:T(8,128)(2,1)S(1)} %get-tuple-element.143), channel_id=1, source_target_pairs={{0,16},{8,24},{16,0},{24,8},{1,17},{9,25},{17,1},{25,9},{2,18},{10... | collective-permute-start | bytes 196616 | tf_op jit(solution)/shard_map/ppermute | solution.py:686
  136.0 6.6 %collective-permute-start.40 = (bf16[64,512]{1,0:T(8,128)(2,1)S(1)}, bf16[64,512]{1,0:T(8,128)(2,1)S(1)}, u32[]{:S(2)}, u32[]{:S(2)}) collective-permute-start(bf16[64,512]{1,0:T(8,128)(2,1)S(1)} %add_convert_fusion.2), channel_id=1, source_target_pairs={{0,24},{8,16},{16,8},{24,0},{1,25},{9,17},{17,9},{25,1},{2,26},{10... | collective-permute-start | bytes 196616 | tf_op jit(solution)/shard_map/ppermute | solution.py:686
  145.4 92.1 %all-gather.15.cloned.1.call-start = ((), (), s32[]{:S(2)}) async-start(), calls=%async_computation.3 | async-start | bytes 4718592 | tf_op jit(solution)/shard_map/all_gather | solution.py:699
  152.9 6.8 %collective-permute-start.41 = (bf16[128,512]{1,0:T(8,128)(2,1)S(1)}, bf16[128,512]{1,0:T(8,128)(2,1)S(1)}, u32[]{:S(2)}, u32[]{:S(2)}) collective-permute-start(bf16[128,512]{1,0:T(8,128)(2,1)S(1)} %get-tuple-element.152), channel_id=1, source_target_pairs={{0,8},{8,0},{16,24},{24,16},{1,9},{9,1},{17,25},{25,17},{2,10},{10... | collective-permute-start | bytes 393224 | tf_op jit(solution)/shard_map/ppermute | solution.py:686
  153.1 12.7 %collective-permute-start.42 = (bf16[128,512]{1,0:T(8,128)(2,1)S(1)}, bf16[128,512]{1,0:T(8,128)(2,1)S(1)}, u32[]{:S(2)}, u32[]{:S(2)}) collective-permute-start(bf16[128,512]{1,0:T(8,128)(2,1)S(1)} %get-tuple-element.153), channel_id=1, source_target_pairs={{0,16},{8,24},{16,0},{24,8},{1,17},{9,25},{17,1},{25,9},{2,18},{10... | collective-permute-start | bytes 393224 | tf_op jit(solution)/shard_map/ppermute | solution.py:686
  155.2 10.6 %collective-permute-start.43 = (bf16[128,512]{1,0:T(8,128)(2,1)S(1)}, bf16[128,512]{1,0:T(8,128)(2,1)S(1)}, u32[]{:S(2)}, u32[]{:S(2)}) collective-permute-start(bf16[128,512]{1,0:T(8,128)(2,1)S(1)} %get-tuple-element.154), channel_id=1, source_target_pairs={{0,24},{8,16},{16,8},{24,0},{1,25},{9,17},{17,9},{25,1},{2,26},{10... | collective-permute-start | bytes 393224 | tf_op jit(solution)/shard_map/ppermute | solution.py:686
  165.9 8.2 %collective-permute-start.46 = (bf16[128,512]{1,0:T(8,128)(2,1)S(1)}, bf16[128,512]{1,0:T(8,128)(2,1)S(1)}, u32[]{:S(2)}, u32[]{:S(2)}) collective-permute-start(bf16[128,512]{1,0:T(8,128)(2,1)S(1)} %add_convert_fusion.1), channel_id=1, source_target_pairs={{0,24},{8,16},{16,8},{24,0},{1,25},{9,17},{17,9},{25,1},{2,26},{10... | collective-permute-start | bytes 393224 | tf_op jit(solution)/shard_map/ppermute | solution.py:686
  167.3 11.3 %collective-permute-start.45 = (bf16[128,512]{1,0:T(8,128)(2,1)S(1)}, bf16[128,512]{1,0:T(8,128)(2,1)S(1)}, u32[]{:S(2)}, u32[]{:S(2)}) collective-permute-start(bf16[128,512]{1,0:T(8,128)(2,1)S(1)} %add_convert_fusion.1), channel_id=1, source_target_pairs={{0,16},{8,24},{16,0},{24,8},{1,17},{9,25},{17,1},{25,9},{2,18},{10... | collective-permute-start | bytes 393224 | tf_op jit(solution)/shard_map/ppermute | solution.py:686
  169.4 9.2 %collective-permute-start.44 = (bf16[128,512]{1,0:T(8,128)(2,1)S(1)}, bf16[128,512]{1,0:T(8,128)(2,1)S(1)}, u32[]{:S(2)}, u32[]{:S(2)}) collective-permute-start(bf16[128,512]{1,0:T(8,128)(2,1)S(1)} %add_convert_fusion.1), channel_id=1, source_target_pairs={{0,8},{8,0},{16,24},{24,16},{1,9},{9,1},{17,25},{25,17},{2,10},{10... | collective-permute-start | bytes 393224 | tf_op jit(solution)/shard_map/ppermute | solution.py:686
  179.6 81.7 %all-gather.17.cloned.1.call-start = ((), (), s32[]{:S(2)}) async-start(), calls=%async_computation.4 | async-start | bytes 7077888 | tf_op jit(solution)/shard_map/all_gather | solution.py:699
  179.7 8.5 %collective-permute-start.47 = (bf16[192,512]{1,0:T(8,128)(2,1)}, bf16[192,512]{1,0:T(8,128)(2,1)S(1)}, u32[]{:S(2)}, u32[]{:S(2)}) collective-permute-start(bf16[192,512]{1,0:T(8,128)(2,1)} %get-tuple-element.159), channel_id=1, source_target_pairs={{0,8},{8,0},{16,24},{24,16},{1,9},{9,1},{17,25},{25,17},{2,10},{10... | collective-permute-start | bytes 589832 | tf_op jit(solution)/shard_map/ppermute | solution.py:686
  179.8 17.0 %collective-permute-start.48 = (bf16[192,512]{1,0:T(8,128)(2,1)}, bf16[192,512]{1,0:T(8,128)(2,1)S(1)}, u32[]{:S(2)}, u32[]{:S(2)}) collective-permute-start(bf16[192,512]{1,0:T(8,128)(2,1)} %get-tuple-element.160), channel_id=1, source_target_pairs={{0,16},{8,24},{16,0},{24,8},{1,17},{9,25},{17,1},{25,9},{2,18},{10... | collective-permute-start | bytes 589832 | tf_op jit(solution)/shard_map/ppermute | solution.py:686
  181.5 15.3 %collective-permute-start.49 = (bf16[192,512]{1,0:T(8,128)(2,1)S(1)}, bf16[192,512]{1,0:T(8,128)(2,1)S(1)}, u32[]{:S(2)}, u32[]{:S(2)}) collective-permute-start(bf16[192,512]{1,0:T(8,128)(2,1)S(1)} %copy-done.50), channel_id=1, source_target_pairs={{0,24},{8,16},{16,8},{24,0},{1,25},{9,17},{17,9},{25,1},{2,26},{10... | collective-permute-start | bytes 589832 | tf_op jit(solution)/shard_map/ppermute | solution.py:686
  196.9 11.7 %collective-permute-start.52 = (bf16[192,512]{1,0:T(8,128)(2,1)S(1)}, bf16[192,512]{1,0:T(8,128)(2,1)S(1)}, u32[]{:S(2)}, u32[]{:S(2)}) collective-permute-start(bf16[192,512]{1,0:T(8,128)(2,1)S(1)} %add_convert_fusion), channel_id=1, source_target_pairs={{0,24},{8,16},{16,8},{24,0},{1,25},{9,17},{17,9},{25,1},{2,26},{10... | collective-permute-start | bytes 589832 | tf_op jit(solution)/shard_map/ppermute | solution.py:686
  198.8 17.7 %collective-permute-start.51 = (bf16[192,512]{1,0:T(8,128)(2,1)S(1)}, bf16[192,512]{1,0:T(8,128)(2,1)S(1)}, u32[]{:S(2)}, u32[]{:S(2)}) collective-permute-start(bf16[192,512]{1,0:T(8,128)(2,1)S(1)} %add_convert_fusion), channel_id=1, source_target_pairs={{0,16},{8,24},{16,0},{24,8},{1,17},{9,25},{17,1},{25,9},{2,18},{10... | collective-permute-start | bytes 589832 | tf_op jit(solution)/shard_map/ppermute | solution.py:686
  208.6 7.9 %collective-permute-start.50 = (bf16[192,512]{1,0:T(8,128)(2,1)S(1)}, bf16[192,512]{1,0:T(8,128)(2,1)S(1)}, u32[]{:S(2)}, u32[]{:S(2)}) collective-permute-start(bf16[192,512]{1,0:T(8,128)(2,1)S(1)} %add_convert_fusion), channel_id=1, source_target_pairs={{0,8},{8,0},{16,24},{24,16},{1,9},{9,1},{17,25},{25,17},{2,10},{10... | collective-permute-start | bytes 589832 | tf_op jit(solution)/shard_map/ppermute | solution.py:686
  219.4 7.7 %collective-permute-start.32 = (bf16[288,128]{1,0:T(8,128)(2,1)S(1)}, bf16[288,128]{1,0:T(8,128)(2,1)S(1)}, u32[]{:S(2)}, u32[]{:S(2)}) collective-permute-start(bf16[288,128]{1,0:T(8,128)(2,1)S(1)} %copy-done.33), channel_id=1, source_target_pairs={{0,5},{1,4},{2,7},{3,6},{4,1},{5,0},{6,3},{7,2},{8,13},{9,12},{10,... | collective-permute-start | bytes 221192 | tf_op jit(solution)/shard_map/ppermute | solution.py:686
  222.7 6.6 %collective-permute-start.34 = (bf16[288,128]{1,0:T(8,128)(2,1)S(1)}, bf16[288,128]{1,0:T(8,128)(2,1)S(1)}, u32[]{:S(2)}, u32[]{:S(2)}) collective-permute-start(bf16[288,128]{1,0:T(8,128)(2,1)S(1)} %get-tuple-element.137), channel_id=1, source_target_pairs={{0,7},{1,6},{2,5},{3,4},{4,3},{5,2},{6,1},{7,0},{8,15},{9,14},{10,... | collective-permute-start | bytes 221192 | tf_op jit(solution)/shard_map/ppermute | solution.py:686
  (83 other events, 1017.1 us)
Sparse Core Ops, SparseCore 0:
  17.1 38.6 all-gather.8
  58.2 26.2 all-gather.10
  145.5 25.3 all-gather.12
  179.8 33.6 all-gather.14
  217.6 43.6 all-gather.16
